TPU v7x, 32 devices: a whole 2x2x4 slice. The times are simulated.
32 devices in a mesh: row: 8 (over y, x, core), col: 4 (over z).
Axes of the slice: x: 2, y: 2, z: 4, core: 2. Of those that a mesh axis runs over, the one named last changes fastest.
Arguments:
- tokens: int32 [256], replicated, may hold values from 0 to 8191
- emission_table: bfloat16 [8192, 32768], P('row', 'col'), may hold values from -3 to 0
- forward_rows: bfloat16 [256, 32768], P('col', 'row'), may hold values from 0.05 to 64
- backward_rows: bfloat16 [256, 32768], P('row', 'col'), may hold values from 0.05 to 64
- src_embed: bfloat16 [32768, 256], P(('row', 'col')), may hold values from -12 to 12
- tgt_embed: bfloat16 [32768, 256], P(('col', 'row')), may hold values from -12 to 12
Outputs:
- grad_src: float32 [32768, 256], P(('row', 'col'))
- grad_tgt: float32 [32768, 256], P(('col', 'row'))
All inputs are finite; a program needn't handle non-finite values.
Results may differ from a plain program's by a relative error of at most 0.018.
Values may be sent and summed in bfloat16 or wider, within the bound.
A program may use at most 384 MiB of HBM per device.

v0:
```python
import jax
import jax.numpy as jnp
from jax import lax
from jax.sharding import PartitionSpec as P

S = 32768
SEQS = 256


def on_device(tokens, emission_table, forward_rows, backward_rows, src_embed, tgt_embed):
    src_block = lax.all_gather(src_embed, "col", axis=0, tiled=True)
    tgt_block = lax.all_gather(tgt_embed, "row", axis=0, tiled=True)
    forward_all = lax.all_gather(forward_rows, "col", axis=0, tiled=True).astype(jnp.float32)
    logits = lax.dot_general(
        src_block, tgt_block, (((1,), (1,)), ((), ())), preferred_element_type=jnp.float32
    )
    row_peak = lax.pmax(jnp.max(logits, axis=1), "col")
    exp_full = jnp.exp(logits - row_peak[:, None])
    local_sums = jnp.sum(exp_full, axis=1)
    exp_block = exp_full.astype(jnp.bfloat16)
    vocab_local = emission_table.shape[0]
    offset = lax.axis_index("row") * vocab_local
    onehot = (tokens[:, None] == offset + jnp.arange(vocab_local, dtype=jnp.int32)[None, :]).astype(
        jnp.bfloat16
    )
    looked = jnp.dot(onehot, emission_table, preferred_element_type=jnp.float32)
    summed_looks = lax.psum(looked.astype(jnp.bfloat16), "row").astype(jnp.float32)
    backward_all = lax.all_gather(backward_rows, "row", axis=0, tiled=True)
    weighted = (jnp.exp(summed_looks) * backward_all.astype(jnp.float32)).astype(jnp.bfloat16)
    local_reach = lax.dot_general(
        weighted, exp_block, (((1,), (1,)), ((), ())), preferred_element_type=jnp.float32
    )
    row_sums, reach = lax.psum((local_sums, local_reach), "col")
    local_norm = jnp.sum(forward_all * reach / row_sums[None, :], axis=1)
    norm_terms = lax.psum(local_norm, "row")
    factor = jnp.float32(S) / jnp.float32(SEQS)
    coeffs = (factor * forward_all / (norm_terms[:, None] * row_sums[None, :])).astype(jnp.bfloat16)
    summed = lax.dot_general(
        coeffs, weighted, (((0,), (0,)), ((), ())), preferred_element_type=jnp.float32
    )
    exp_wide = exp_block.astype(jnp.float32)
    counts = exp_wide * summed
    row_counts = lax.psum(jnp.sum(counts, axis=1), "col")
    grad_logits = (counts - exp_wide * (row_counts / row_sums)[:, None]).astype(jnp.bfloat16)
    piece = grad_logits
    grad_src = lax.psum_scatter(
        jnp.dot(piece, tgt_block, preferred_element_type=jnp.float32),
        "col",
        scatter_dimension=0,
        tiled=True,
    )
    piece = grad_logits
    grad_tgt = lax.psum_scatter(
        lax.dot_general(
            piece, src_block, (((0,), (0,)), ((), ())), preferred_element_type=jnp.float32
        ),
        "row",
        scatter_dimension=0,
        tiled=True,
    )
    return (grad_src, grad_tgt)


def solution(mesh):
    in_specs = (
        P(),
        P("row", "col"),
        P("col", "row"),
        P("row", "col"),
        P(("row", "col"), None),
        P(("col", "row"), None),
    )
    out_specs = (P(("row", "col"), None), P(("col", "row"), None))
    return jax.shard_map(
        on_device, mesh=mesh, in_specs=in_specs, out_specs=out_specs, check_vma=False
    )
```

profile of v0, /device:TPU:8, one launch (start us, length us, event | category | flops | bytes accessed | tf_op | source)
XLA Modules:
  0.0 794.1 jit_solution(203490441518982156)
XLA Ops:
  7.2 0.0 all-gather.5.cloned.1.call-start
  7.2 0.7 all-gather.5.cloned.1.call-update
  7.9 0.0 all-gather.7.cloned.1.call-start
  7.9 0.7 all-gather.7.cloned.1.call-update
  8.6 0.0 all-reduce.3.cloned.1.call-start
  8.7 11.9 %convolution_convert_fusion = bf16[256,8192]{1,0:T(8,128)(2,1)} fusion(bf16[1024,8192]{1,0:T(8,128)(2,1)} %param.7, s32[1024]{0:T(1024)S(1)} %iota_add_fusion, s32[256]{0:T(256)} %param.6), kind=kOutput, calls=%fused_computation.8 | convolution fusion | flops 4297326592 | bytes 20976640 | tf_op jit(solution)/shard_map/dot_general | solution.py:26
  20.6 0.0 all-reduce.3.cloned.1.call-update
  20.6 0.0 all-gather.11.cloned.1.call-start
  20.7 0.5 all-gather.11.cloned.1.call-update
  21.2 0.0 all-gather.9.cloned.1.call-start
  21.3 0.5 all-gather.9.cloned.1.call-update
  21.8 0.0 all-reduce.5.cloned.1.call-start
  21.9 33.2 %all-gather.5.cloned.1.call-done = bf16[4096,256]{1,0:T(8,128)(2,1)} async-done(((bf16[1024,256]{1,0:T(8,128)(2,1)}), bf16[4096,256]{1,0:T(8,128)(2,1)}) %all-gather.5.cloned.1.call-update) | async-done | bytes 2097168 | tf_op jit(solution)/shard_map/all_gather | solution.py:11
  55.1 39.0 %all-gather.7.cloned.1.call-done = bf16[8192,256]{1,0:T(8,128)(2,1)} async-done(((bf16[1024,256]{1,0:T(8,128)(2,1)}), bf16[8192,256]{1,0:T(8,128)(2,1)}) %all-gather.7.cloned.1.call-update) | async-done | bytes 4194320 | tf_op jit(solution)/shard_map/all_gather | solution.py:12
  94.0 50.6 %fusion.19 = (f32[4096]{0:T(1024)S(1)}, f32[4096,8192]{1,0:T(8,128)}) fusion(bf16[4096,256]{1,0:T(8,128)(2,1)} %all-gather.5.cloned.1.call-done, bf16[8192,256]{1,0:T(8,128)(2,1)} %all-gather.7.cloned.1.call-done), kind=kOutput, calls=%fused_computation.26 | convolution fusion | flops 17213419520 | bytes 140525568 | tf_op jit(solution)/shard_map/dot_general | solution.py:14
  144.7 15.2 %pmax.7 = f32[4096]{0:T(1024)S(1)} all-reduce(f32[4096]{0:T(1024)S(1)} %get-tuple-element.4), channel_id=1, replica_groups=mesh['row'=8,'col'=4] {'col'}, use_global_device_ids=true, to_apply=%region_1.0 | all-reduce | flops 4096 | bytes 32768 | tf_op jit(solution)/shard_map/pmax | solution.py:17
  159.8 65.9 %fusion.2 = (f32[4096]{0:T(1024)S(1)}, bf16[4096,8192]{1,0:T(8,128)(2,1)}) fusion(f32[4096,8192]{1,0:T(8,128)} %get-tuple-element.5, f32[4096]{0:T(1024)S(1)} %pmax.7), kind=kLoop, calls=%fused_computation.5 | loop fusion | flops 100659200 | bytes 201359360 | tf_op jit(solution)/shard_map/reduce_sum | solution.py:19
  225.8 30.6 %fusion.14 = f32[256,4096]{1,0:T(8,128)} fusion(bf16[4096,8192]{1,0:T(8,128)(2,1)} %get-tuple-element.3, bf16[256,8192]{1,0:T(8,128)(2,1)} %all-gather.11.cloned.1.call-done, bf16[256,8192]{1,0:T(8,128)(2,1)} %all-reduce.3.cloned.1.call-done), kind=kOutput, calls=%fused_computation.20 | convolution fusion | flops 17188257792 | bytes 79691776 | tf_op jit(solution)/shard_map/dot_general | solution.py:30
  256.4 0.0 reduce-scatter.3.cloned.1.call-start
  256.4 17.2 %psum.37 = f32[4096]{0:T(1024)S(1)} all-reduce(f32[4096]{0:T(1024)S(1)} %get-tuple-element.2), channel_id=1, replica_groups=mesh['row'=8,'col'=4] {'col'}, use_global_device_ids=true, to_apply=%region_5.0 | all-reduce | flops 4096 | bytes 32768 | tf_op jit(solution)/shard_map/psum | solution.py:33
  273.7 145.0 %all-reduce.5.cloned.1.call-done = f32[256,4096]{1,0:T(8,128)} async-done(((f32[256,4096]{1,0:T(8,128)}), f32[256,4096]{1,0:T(8,128)}) %all-reduce.5.cloned.1.call-update) | async-done | bytes 4194320 | tf_op jit(solution)/shard_map/psum | solution.py:33
  418.7 3.5 fusion.8
  422.2 14.1 %psum.38 = f32[256]{0:T(256)S(1)} all-reduce(f32[256]{0:T(256)S(1)} %fusion.8), channel_id=1, replica_groups=mesh['row'=8,'col'=4] {'row'}, use_global_device_ids=true, to_apply=%region_7.0 | all-reduce | flops 256 | bytes 2048 | tf_op jit(solution)/shard_map/psum | solution.py:35
  436.3 71.2 %fusion.4 = (f32[4096]{0:T(1024)S(1)}, f32[4096,8192]{1,0:T(8,128)}) fusion(bf16[4096,8192]{1,0:T(8,128)(2,1)} %get-tuple-element.3, bf16[256,8192]{1,0:T(8,128)(2,1)} %all-gather.11.cloned.1.call-done, bf16[256,8192]{1,0:T(8,128)(2,1)} %all-reduce.3.cloned.1.call-done, bf16[256,4096]{1,0:T(8,128)(2,1)S(1)} %copy-done, f32[256]{0:T(256)S(1)} %psum.38, ...), kind=kOutput, calls=%fused_computation.7 | convolution fusion | flops 17294159872 | bytes 211846144 | tf_op jit(solution)/shard_map/dot_general | solution.py:38
  507.4 16.0 %psum.39 = f32[4096]{0:T(1024)S(1)} all-reduce(f32[4096]{0:T(1024)S(1)} %get-tuple-element.6), channel_id=1, replica_groups=mesh['row'=8,'col'=4] {'col'}, use_global_device_ids=true, to_apply=%region_9.0 | all-reduce | flops 4096 | bytes 32768 | tf_op jit(solution)/shard_map/psum | solution.py:43
  523.5 83.2 %fusion.1 = bf16[4096,8192]{1,0:T(8,128)(2,1)} fusion(bf16[4096,8192]{1,0:T(8,128)(2,1)} %get-tuple-element.3, f32[4096,8192]{1,0:T(8,128)} %get-tuple-element.7, f32[4096]{0:T(1024)S(1)} %div.17), kind=kLoop, calls=%fused_computation.3 | loop fusion | flops 167772160 | bytes 268451840 | tf_op jit(solution)/shard_map/convert_element_type | solution.py:44
  606.7 28.3 %fusion.20 = f32[4096,256]{1,0:T(8,128)} fusion(bf16[4096,8192]{1,0:T(8,128)(2,1)} %fusion.1, bf16[8192,256]{1,0:T(8,128)(2,1)} %all-gather.7.cloned.1.call-done), kind=kOutput, calls=%fused_computation.27 | convolution fusion | flops 17179869184 | bytes 75497472 | tf_op jit(solution)/shard_map/dot_general | solution.py:47
  635.0 0.0 reduce-scatter.5.cloned.1.call-start
  635.0 1.5 copy-done.1
  636.5 30.2 %fusion.21 = f32[8192,256]{1,0:T(8,128)} fusion(bf16[4096,8192]{1,0:T(8,128)(2,1)} %fusion.1, bf16[4096,256]{1,0:T(8,128)(2,1)S(1)} %copy-done.1), kind=kOutput, calls=%fused_computation.28 | convolution fusion | flops 17179869184 | bytes 77594624 | tf_op jit(solution)/shard_map/dot_general | solution.py:54
  666.7 44.2 %reduce-scatter.3.cloned.1.call-done = f32[1024,256]{1,0:T(8,128)} async-done(((f32[4096,256]{1,0:T(8,128)}), f32[1024,256]{1,0:T(8,128)}) %reduce-scatter.3.cloned.1.call-update) | async-done | bytes 1048592 | tf_op jit(solution)/shard_map/reduce_scatter | solution.py:46
  711.0 76.3 %reduce-scatter.5.cloned.1.call-done = f32[1024,256]{1,0:T(8,128)} async-done(((f32[8192,256]{1,0:T(8,128)}), f32[1024,256]{1,0:T(8,128)}) %reduce-scatter.5.cloned.1.call-update) | async-done | bytes 1048592 | tf_op jit(solution)/shard_map/reduce_scatter | solution.py:53
  (11 shorter events, 0.1 us)
Async XLA Ops:
  7.2 47.9 %all-gather.5.cloned.1.call-start = ((), (), s32[]{:S(2)}) async-start(), calls=%async_computation.2 | async-start | bytes 2621440 | tf_op jit(solution)/shard_map/all_gather | solution.py:11
  7.9 86.2 %all-gather.7.cloned.1.call-start = ((), (), s32[]{:S(2)}) async-start(), calls=%async_computation.3 | async-start | bytes 4718592 | tf_op jit(solution)/shard_map/all_gather | solution.py:12
  8.6 217.1 %all-reduce.3.cloned.1.call-start = ((), (), s32[]{:S(2)}) async-start(), calls=%async_computation.5 | async-start | bytes 8388608 | tf_op jit(solution)/shard_map/psum | solution.py:27
  20.6 205.1 %all-gather.11.cloned.1.call-start = ((), (), s32[]{:S(2)}) async-start(), calls=%async_computation.6 | async-start | bytes 4718592 | tf_op jit(solution)/shard_map/all_gather | solution.py:28
  21.2 252.4 %all-gather.9.cloned.1.call-start = ((), (), s32[]{:S(2)}) async-start(), calls=%async_computation.4 | async-start | bytes 2621440 | tf_op jit(solution)/shard_map/all_gather | solution.py:13
  21.8 396.9 %all-reduce.5.cloned.1.call-start = ((), (), s32[]{:S(2)}) async-start(), calls=%async_computation.7 | async-start | bytes 8388608 | tf_op jit(solution)/shard_map/psum | solution.py:33
  256.4 454.6 %reduce-scatter.3.cloned.1.call-start = ((), (), s32[]{:S(2)}) async-start(), calls=%async_computation.8 | async-start | bytes 5242880 | tf_op jit(solution)/shard_map/reduce_scatter | solution.py:46
  273.7 162.6 %copy-start = (bf16[256,4096]{1,0:T(8,128)(2,1)S(1)}, bf16[256,4096]{1,0:T(8,128)(2,1)}, u32[]{:S(2)}) copy-start(bf16[256,4096]{1,0:T(8,128)(2,1)} %all-gather.9.cloned.1.call-done) | copy-start | bytes 6291460
  634.9 1.6 copy-start.1
  635.0 152.3 %reduce-scatter.5.cloned.1.call-start = ((), (), s32[]{:S(2)}) async-start(), calls=%async_computation.9 | async-start | bytes 9437184 | tf_op jit(solution)/shard_map/reduce_scatter | solution.py:53
Sparse Core Ops, SparseCore 0:
  9.6 45.4 all-gather.4
  57.0 37.0 all-gather.6
  97.3 81.0 all-reduce.2
  180.3 36.7 all-gather.10
  218.6 44.3 all-gather.8
  265.4 153.2 all-reduce.4
  635.1 75.8 reduce-scatter.2
  715.4 71.7 reduce-scatter.4
where the time goes:
time: 796 us; the launch traced here: 794 us
  waiting for transfers between devices  340 us (43%)
  matrix products  223 us (28%)
  other arithmetic  153 us (19%)
  blocking collectives  62.5 us (8%)
  between operations  14.2 us (2%)
    psum x1, waiting for transfers between devices, on_device(): row_sums, reach = lax.psum((local_sums, local_reach), 'col')  145 us
    convert_element_type x1, other arithmetic, on_device(): (counts - exp_wide * (row_counts / row_sums)[:, None]).astype(jnp.bfloat16)  83.2 us
    reduce_scatter x1, waiting for transfers between devices, on_device(): lax.psum_scatter(lax.dot_general(piece, src_block, (((0,), (0,)), ((), ()...  76.3 us
    dot_general x1, matrix products, on_device(): lax.dot_general(coeffs, weighted, (((0,), (0,)), ((), ())), preferred_ele...  71.2 us
    reduce_sum x1, other arithmetic, on_device(): local_sums = jnp.sum(exp_full, axis=1)  65.9 us
    dot_general x1, matrix products, on_device(): lax.dot_general(src_block, tgt_block, (((1,), (1,)), ((), ())), preferred...  50.6 us
    reduce_scatter x1, waiting for transfers between devices, on_device(): lax.psum_scatter(jnp.dot(piece, tgt_block, preferred_element_type=jnp.flo...  44.2 us
    all_gather x1, waiting for transfers between devices, on_device(): tgt_block = lax.all_gather(tgt_embed, 'row', axis=0, tiled=True)  39 us
  transfers between devices with their start and end apart: 8, of which 5 were waited for; matrix products, arithmetic and copies ran while one was open for 24% of the time, Pallas kernels for 0%

commit v1 on v0

v1 whole, which is shorter than its diff:
```python
import jax
import jax.numpy as jnp
from jax import lax
from jax.experimental import pallas as pl
from jax.experimental.pallas import tpu as pltpu
from jax.sharding import PartitionSpec as P

S = 32768
SEQS = 256
NT = (((1,), (1,)), ((), ()))
BF16 = jnp.bfloat16
F32 = jnp.float32


def fit(size, want):
    while size % want:
        want //= 2
    return want


def first_pass(src, tgt, weighted):
    rows, width = src.shape
    cols = tgt.shape[0]
    seqs = weighted.shape[0]
    tile = fit(rows, 256)
    chunk = fit(cols, 1024)
    tiles = rows // tile

    def body(src_ref, tgt_ref, w_ref, e_ref, reach_ref, sum_ref, peak_ref, s0, s1, p0, p1):
        step = pl.program_id(0)

        def run(new, old, new_peak, old_peak):
            peak = old_peak[...]

            def go(c, carry):
                best, total, reach = carry
                at = pl.ds(pl.multiple_of(c * chunk, chunk), chunk)
                logits = lax.dot_general(src_ref[...], tgt_ref[at, :], NT, preferred_element_type=F32)
                new[:, at] = logits
                best = jnp.maximum(best, jnp.max(logits, axis=1, keepdims=True))
                e = jnp.exp(old[:, at] - peak)
                total = total + jnp.sum(e, axis=1, keepdims=True)
                eb = e.astype(BF16)
                e_ref[:, at] = eb
                reach = reach + lax.dot_general(eb, w_ref[:, at], NT, preferred_element_type=F32)
                return best, total, reach

            best, total, reach = lax.fori_loop(
                0,
                cols // chunk,
                go,
                (jnp.full((tile, 1), -jnp.inf, F32), jnp.zeros((tile, 1), F32), jnp.zeros((tile, seqs), F32)),
            )
            new_peak[...] = best
            reach_ref[...] = reach
            sum_ref[...] = total
            peak_ref[...] = peak

        @pl.when(lax.rem(step, 2) == 0)
        def _():
            run(s0, s1, p0, p1)

        @pl.when(lax.rem(step, 2) == 1)
        def _():
            run(s1, s0, p1, p0)

    ahead = lambda t: (jnp.minimum(t, tiles - 1), 0)
    behind = lambda t: (jnp.maximum(t - 1, 0), 0)
    whole = lambda t: (0, 0)
    return pl.pallas_call(
        body,
        grid=(tiles + 1,),
        in_specs=[
            pl.BlockSpec((tile, width), ahead),
            pl.BlockSpec((cols, width), whole),
            pl.BlockSpec((seqs, cols), whole),
        ],
        out_specs=[
            pl.BlockSpec((tile, cols), behind),
            pl.BlockSpec((tile, seqs), behind),
            pl.BlockSpec((tile, 1), behind),
            pl.BlockSpec((tile, 1), behind),
        ],
        out_shape=[
            jax.ShapeDtypeStruct((rows, cols), BF16),
            jax.ShapeDtypeStruct((rows, seqs), F32),
            jax.ShapeDtypeStruct((rows, 1), F32),
            jax.ShapeDtypeStruct((rows, 1), F32),
        ],
        scratch_shapes=[
            pltpu.VMEM((tile, cols), F32),
            pltpu.VMEM((tile, cols), F32),
            pltpu.VMEM((tile, 1), F32),
            pltpu.VMEM((tile, 1), F32),
        ],
        compiler_params=pltpu.CompilerParams(
            dimension_semantics=("arbitrary",), vmem_limit_bytes=58 * 1024 * 1024
        ),
        cost_estimate=pl.CostEstimate(
            flops=2 * rows * cols * (width + seqs), bytes_accessed=2 * rows * cols, transcendentals=rows * cols
        ),
        name="first_pass",
    )(src, tgt, weighted)


def second_pass(exp_block, coeffs, share, weighted, tgt, src, src_t):
    rows, cols = exp_block.shape
    width = tgt.shape[1]
    seqs = weighted.shape[0]
    tile = fit(rows, 512)
    chunk = fit(cols, 512)
    group = 4 if (cols // chunk) % 4 == 0 else 1

    def body(e_ref, c_ref, share_ref, w_ref, tgt_ref, st_ref, gs_ref, gt_ref):
        first = pl.program_id(0) == 0

        @pl.when(first)
        def _():
            gt_ref[...] = jnp.zeros_like(gt_ref)

        def go(c, total):
            for k in range(group):
                at = pl.ds(pl.multiple_of((c * group + k) * chunk, chunk), chunk)
                summed = jnp.dot(c_ref[...], w_ref[:, at], preferred_element_type=F32)
                g = (e_ref[:, at].astype(F32) * (summed - share_ref[...])).astype(BF16)
                total = total + jnp.dot(g, tgt_ref[at, :], preferred_element_type=F32)
                gt_ref[:, at] += jnp.dot(st_ref[...], g, preferred_element_type=F32)
            return total

        gs_ref[...] = lax.fori_loop(0, cols // chunk // group, go, jnp.zeros((tile, width), F32))

    by_row = lambda t: (t, 0)
    whole = lambda t: (0, 0)
    return pl.pallas_call(
        body,
        grid=(rows // tile,),
        in_specs=[
            pl.BlockSpec((tile, cols), by_row),
            pl.BlockSpec((tile, seqs), by_row),
            pl.BlockSpec((tile, 1), by_row),
            pl.BlockSpec((seqs, cols), whole, pipeline_mode=pl.Buffered(1)),
            pl.BlockSpec((cols, width), whole, pipeline_mode=pl.Buffered(1)),
            pl.BlockSpec((width, tile), lambda t: (0, t)),
        ],
        out_specs=[
            pl.BlockSpec((tile, width), by_row),
            pl.BlockSpec((width, cols), whole, pipeline_mode=pl.Buffered(1)),
        ],
        out_shape=[
            jax.ShapeDtypeStruct((rows, width), F32),
            jax.ShapeDtypeStruct((width, cols), F32),
        ],
        compiler_params=pltpu.CompilerParams(
            dimension_semantics=("arbitrary",), vmem_limit_bytes=58 * 1024 * 1024
        ),
        cost_estimate=pl.CostEstimate(
            flops=2 * rows * cols * (2 * width + seqs), bytes_accessed=2 * rows * cols, transcendentals=0
        ),
        name="second_pass",
    )(exp_block, coeffs, share, weighted, tgt, src_t)


def on_device(tokens, emission_table, forward_rows, backward_rows, src_embed, tgt_embed):
    src_block = lax.all_gather(src_embed, "col", axis=0, tiled=True)
    tgt_block = lax.all_gather(tgt_embed, "row", axis=0, tiled=True)
    vocab_local = emission_table.shape[0]
    offset = lax.axis_index("row") * vocab_local
    onehot = (tokens[:, None] == offset + jnp.arange(vocab_local, dtype=jnp.int32)[None, :]).astype(BF16)
    looked = jnp.dot(onehot, emission_table, preferred_element_type=F32).astype(BF16)
    mine = lax.psum_scatter(looked, "row", scatter_dimension=0, tiled=True).astype(F32)
    weighted = (jnp.exp(mine) * backward_rows.astype(F32)).astype(BF16)
    weighted = lax.all_gather(weighted, "row", axis=0, tiled=True)
    forward_all = lax.all_gather(forward_rows.T, "col", axis=1, tiled=True).astype(F32)

    exp_block, reach, local_sums, local_peak = first_pass(src_block, tgt_block, weighted)

    row_peak = lax.pmax(local_peak, "col")
    scale = jnp.exp(local_peak - row_peak)
    row_sums = lax.psum(local_sums * scale, "col")
    reach = reach * scale
    norm_terms = lax.psum(jnp.sum(forward_all * reach / row_sums, axis=0, keepdims=True), ("row", "col"))
    factor = F32(S) / F32(SEQS)
    coeffs = (factor * forward_all / (norm_terms * row_sums)).astype(BF16)
    row_counts = lax.psum(jnp.sum(coeffs.astype(F32) * reach, axis=1, keepdims=True), "col")
    share = row_counts / row_sums * scale
    coeffs = (coeffs.astype(F32) * scale).astype(BF16)

    part_src, part_tgt = second_pass(
        exp_block, coeffs, share, weighted, tgt_block, src_block, src_block.T
    )
    grad_src = lax.psum_scatter(part_src, "col", scatter_dimension=0, tiled=True)
    grad_tgt = lax.psum_scatter(part_tgt, "row", scatter_dimension=1, tiled=True).T
    return (grad_src, grad_tgt)


def solution(mesh):
    in_specs = (
        P(),
        P("row", "col"),
        P("col", "row"),
        P("row", "col"),
        P(("row", "col"), None),
        P(("col", "row"), None),
    )
    out_specs = (P(("row", "col"), None), P(("col", "row"), None))
    return jax.shard_map(
        on_device, mesh=mesh, in_specs=in_specs, out_specs=out_specs, check_vma=False
    )
```

time: 796 us -> 803 us (level)
  matrix products: 223 us -> 11.9 us
  blocking collectives: 62.5 us -> 263 us
  Pallas kernels: 0 us -> 163 us
  other arithmetic: 153 us -> 22.2 us
  waiting for transfers between devices: 340 us -> 311 us
  local copies, waits for them, and re-layouts: 1.52 us -> 13.3 us
    dot_general x6 -> x1, matrix products: 223 us -> 11.9 us  [on_device(): jnp.dot(onehot, emission_table, preferred_element_type=F32).astype(BF16)]
    pallas_call x0 -> x2, Pallas kernels: none -> 163 us  [the longest x1 91.4 us: first_pass(): pl.pallas_call(body, grid=(tiles + 1,), in_specs=[pl.BlockSpec((tile, wid...]
    psum x2 -> x0, waiting for transfers between devices: 145 us -> none  [the longest x1 145 us: on_device(): row_sums, reach = lax.psum((local_sums, local_reach), 'col')]
    psum x3, blocking collectives: 47.3 us -> 188 us  [the longest x1 74.6 us: on_device(): row_sums = lax.psum(local_sums * scale, 'col')]
    convert_element_type x1, other arithmetic: 83.2 us -> 2.03 us  [on_device(): weighted = (jnp.exp(mine) * backward_rows.astype(F32)).astype(BF16)]
    reduce_scatter x2 -> x3, waiting for transfers between devices: 120 us -> 199 us  [the longest x1 77.1 us: on_device(): lax.psum_scatter(part_src, 'col', scatter_dimension=0, tiled=True)]
    reduce_sum x2, other arithmetic: 69.4 us -> 8.51 us  [the longest x1 4.33 us: on_device(): jnp.sum(coeffs.astype(F32) * reach, axis=1, keepdims=True)]
    pmax x1, blocking collectives: 15.2 us -> 75.5 us  [on_device(): row_peak = lax.pmax(local_peak, 'col')]
  transfers between devices with their start and end apart: 8 -> 7, of which waited for: 5 -> 6; matrix products, arithmetic and copies ran while one was open for 24% -> 2% of each run, Pallas kernels for 0% -> 0%
where the time goes in v1:
time: 803 us; the launch traced here: 801 us
  waiting for transfers between devices  311 us (39%)
  blocking collectives  263 us (33%)
  Pallas kernels  163 us (20%)
  other arithmetic  22.2 us (3%)
  between operations  15.5 us (2%)
  local copies, waits for them, and re-layouts  13.3 us (2%)
  matrix products  11.9 us (1%)
    pallas_call x1, Pallas kernels, first_pass(): pl.pallas_call(body, grid=(tiles + 1,), in_specs=[pl.BlockSpec((tile, wid...  91.4 us
    reduce_scatter x1, waiting for transfers between devices, on_device(): lax.psum_scatter(part_src, 'col', scatter_dimension=0, tiled=True)  77.1 us
    pmax x1, blocking collectives, on_device(): row_peak = lax.pmax(local_peak, 'col')  75.5 us
    psum x1, blocking collectives, on_device(): row_sums = lax.psum(local_sums * scale, 'col')  74.6 us
    psum x1, blocking collectives, on_device(): lax.psum(jnp.sum(coeffs.astype(F32) * reach, axis=1, keepdims=True), 'col')  73.4 us
    reduce_scatter x1, waiting for transfers between devices, on_device(): lax.psum_scatter(part_tgt, 'row', scatter_dimension=1, tiled=True)  72.4 us
    pallas_call x1, Pallas kernels, second_pass(): pl.pallas_call(body, grid=(rows // tile,), in_specs=[pl.BlockSpec((tile,...  71.9 us
    reduce_scatter x1, waiting for transfers between devices, on_device(): lax.psum_scatter(looked, 'row', scatter_dimension=0, tiled=True).astype(F32)  50 us
  transfers between devices with their start and end apart: 7, of which 6 were waited for; matrix products, arithmetic and copies ran while one was open for 2% of the time, Pallas kernels for 0%

profile of v1, /device:TPU:8, one launch (start us, length us, event | category | flops | bytes accessed | tf_op | source)
XLA Modules:
  0.0 801.0 jit_solution(18119979609101707892)
XLA Ops:
  8.1 11.9 %convolution_convert_fusion = bf16[256,8192]{1,0:T(8,128)(2,1)} fusion(bf16[1024,8192]{1,0:T(8,128)(2,1)} %param.7, s32[1024]{0:T(1024)S(1)} %iota_add_fusion, s32[256]{0:T(256)} %param.6), kind=kOutput, calls=%fused_computation | convolution fusion | flops 4297326592 | bytes 20976640 | tf_op jit(solution)/shard_map/dot_general | solution.py:169
  20.0 0.0 all-gather.11.cloned.1.call-start
  20.0 0.5 all-gather.11.cloned.1.call-update
  20.6 0.4 copy-done.2
  21.0 1.0 copy.17
  22.0 0.0 all-gather.7.cloned.1.call-start
  22.1 0.5 all-gather.7.cloned.1.call-update
  22.6 50.0 %reduce-scatter.4.cloned.1.call-done = bf16[32,8192]{1,0:T(8,128)(2,1)} async-done(((bf16[256,8192]{1,0:T(8,128)(2,1)}), bf16[32,8192]{1,0:T(8,128)(2,1)}) %reduce-scatter.4.cloned.1.call-update) | async-done | bytes 524304 | tf_op jit(solution)/shard_map/reduce_scatter | solution.py:170
  72.6 2.0 multiply_convert_fusion
  74.6 0.0 reduce-scatter.8.cloned.1.call-start
  74.7 3.3 copy.19
  78.1 35.9 %all-gather.5.cloned.1.call-done = bf16[4096,256]{0,1:T(8,128)(2,1)} async-done(((bf16[1024,256]{0,1:T(8,128)(2,1)}), bf16[4096,256]{0,1:T(8,128)(2,1)}) %all-gather.5.cloned.1.call-update) | async-done | bytes 2097168 | tf_op jit(solution)/shard_map/all_gather | solution.py:164
  114.0 4.1 copy.18.src_ref
  118.0 34.6 %all-gather.7.cloned.1.call-done.tgt_ref = bf16[8192,256]{1,0:T(8,128)(2,1)} async-done(((bf16[1024,256]{1,0:T(8,128)(2,1)}), bf16[8192,256]{1,0:T(8,128)(2,1)}) %all-gather.7.cloned.1.call-update) | async-done | bytes 4194320 | tf_op jit(solution)/shard_map/all_gather | solution.py:165
  152.6 39.2 %all-gather.9.cloned.1.call-done.w_ref = bf16[256,8192]{1,0:T(8,128)(2,1)} async-done(((bf16[32,8192]{1,0:T(8,128)(2,1)}), bf16[256,8192]{1,0:T(8,128)(2,1)}) %all-gather.9.cloned.1.call-update) | async-done | bytes 4194320 | tf_op jit(solution)/shard_map/all_gather | solution.py:172
  191.8 91.4 %first_pass.1 = (bf16[4096,8192]{1,0:T(8,128)(2,1)}, f32[4096,256]{1,0:T(8,128)}, f32[4096,1]{1,0:T(8,128)}, f32[4096,1]{1,0:T(8,128)}) custom-call(bf16[4096,256]{1,0:T(8,128)(2,1)} %copy.18.src_ref, bf16[8192,256]{1,0:T(8,128)(2,1)} %all-gather.7.cloned.1.call-done.tgt_ref, bf16[256,8192]{1,0:T(8,128)(2,1)} %all-gather.9.cloned.1.call-done.w_ref), custom_call_target="tpu_custom_call" | custom-call | flops 34359738368 | bytes 67108864 | tf_op jit(solution)/shard_map/first_pass/pallas_call | solution.py:70
  283.2 75.5 %pmax.7 = f32[4096,1]{1,0:T(8,128)} all-reduce(f32[4096,1]{1,0:T(8,128)} %get-tuple-element.10), channel_id=1, replica_groups=mesh['row'=8,'col'=4] {'col'}, use_global_device_ids=true, to_apply=%region_1.0 | all-reduce | flops 4096 | bytes 32768 | tf_op jit(solution)/shard_map/pmax | solution.py:177
  358.8 4.7 fusion.9
  363.5 74.6 %psum.21 = f32[4096,1]{1,0:T(8,128)} all-reduce(f32[4096,1]{1,0:T(8,128)} %get-tuple-element.20), channel_id=1, replica_groups=mesh['row'=8,'col'=4] {'col'}, use_global_device_ids=true, to_apply=%region_2.0 | all-reduce | flops 4096 | bytes 32768 | tf_op jit(solution)/shard_map/psum | solution.py:179
  438.1 2.2 reduce.1
  440.3 4.2 fusion.5
  444.5 40.0 %psum.22 = f32[256]{0:T(256)S(1)} all-reduce(f32[256]{0:T(256)S(1)} %fusion.5), channel_id=1, replica_groups=mesh['row'=8,'col'=4] {'row','col'}, use_global_device_ids=true, to_apply=%region_4.0 | all-reduce | flops 256 | bytes 2048 | tf_op jit(solution)/shard_map/psum | solution.py:181
  484.4 4.3 fusion.4
  488.8 2.0 copy.20
  490.8 73.4 %psum.23 = f32[4096,1]{1,0:T(8,128)} all-reduce(f32[4096,1]{1,0:T(8,128)} %copy.20), channel_id=1, replica_groups=mesh['row'=8,'col'=4] {'col'}, use_global_device_ids=true, to_apply=%region_6.0 | all-reduce | flops 4096 | bytes 32768 | tf_op jit(solution)/shard_map/psum | solution.py:184
  564.2 4.8 divide_multiply_fusion.share_ref
  568.9 71.9 %second_pass.1 = (f32[4096,256]{1,0:T(8,128)}, f32[256,8192]{1,0:T(8,128)}) custom-call(bf16[4096,8192]{1,0:T(8,128)(2,1)} %get-tuple-element.8.e_ref, bf16[4096,256]{1,0:T(8,128)(2,1)} %get-tuple-element.23.c_ref, f32[4096,1]{1,0:T(8,128)} %divide_multiply_fusion.share_ref, bf16[256,8192]{1,0:T(8,128)(2,1)} %all-gather.9.cloned.1.call-done.w_ref, ...), custom_call_target="tpu_custom_call" | custom-call | flops 51539607552 | bytes 67108864 | tf_op jit(solution)/shard_map/second_pass/pallas_call | solution.py:134
  640.8 0.0 reduce-scatter.6.cloned.1.call-start
  640.9 0.7 reduce-scatter.6.cloned.1.call-update
  641.6 72.4 %reduce-scatter.8.cloned.1.call-done = f32[256,1024]{1,0:T(8,128)} async-done(((f32[256,8192]{1,0:T(8,128)}), f32[256,1024]{1,0:T(8,128)}) %reduce-scatter.8.cloned.1.call-update) | async-done | bytes 1048592 | tf_op jit(solution)/shard_map/reduce_scatter | solution.py:192
  714.0 2.5 copy.21
  716.5 77.1 %reduce-scatter.6.cloned.1.call-done = f32[1024,256]{1,0:T(8,128)} async-done(((f32[4096,256]{1,0:T(8,128)}), f32[1024,256]{1,0:T(8,128)}) %reduce-scatter.6.cloned.1.call-update) | async-done | bytes 1048592 | tf_op jit(solution)/shard_map/reduce_scatter | solution.py:191
  (14 shorter events, 0.2 us)
Async XLA Ops:
  8.0 64.6 %reduce-scatter.4.cloned.1.call-start = ((), (), s32[]{:S(2)}) async-start(), calls=%async_computation.5 | async-start | bytes 4718592 | tf_op jit(solution)/shard_map/reduce_scatter | solution.py:170
  19.9 1.0 copy-start.2
  19.9 52.7 %copy-start.1 = (bf16[32,8192]{1,0:T(8,128)(2,1)S(1)}, bf16[32,8192]{1,0:T(8,128)(2,1)}, u32[]{:S(2)}) copy-start(bf16[32,8192]{1,0:T(8,128)(2,1)} %param.9) | copy-start | bytes 1572868
  20.0 54.8 %all-gather.11.cloned.1.call-start = ((), (), s32[]{:S(2)}) async-start(), calls=%async_computation.7 | async-start | bytes 2621440 | tf_op jit(solution)/shard_map/all_gather | solution.py:173
  20.5 93.4 %all-gather.5.cloned.1.call-start = ((), (), s32[]{:S(2)}) async-start(), calls=%async_computation.3 | async-start | bytes 2621440 | tf_op jit(solution)/shard_map/all_gather | solution.py:164
  22.0 130.6 %all-gather.7.cloned.1.call-start = ((), (), s32[]{:S(2)}) async-start(), calls=%async_computation.4 | async-start | bytes 4718592 | tf_op jit(solution)/shard_map/all_gather | solution.py:165
  22.6 169.3 %all-gather.9.cloned.1.call-start = ((), (), s32[]{:S(2)}) async-start(), calls=%async_computation.6 | async-start | bytes 4718592 | tf_op jit(solution)/shard_map/all_gather | solution.py:172
  74.6 639.3 %reduce-scatter.8.cloned.1.call-start = ((), (), s32[]{:S(2)}) async-start(), calls=%async_computation.9 | async-start | bytes 9437184 | tf_op jit(solution)/shard_map/reduce_scatter | solution.py:192
  488.8 75.4 %copy-start = (f32[4096,1]{1,0:T(8,128)S(1)}, f32[4096,1]{1,0:T(8,128)}, u32[]{:S(2)}) copy-start(f32[4096,1]{1,0:T(8,128)} %psum.21) | copy-start | bytes 49156
  640.8 152.8 %reduce-scatter.6.cloned.1.call-start = ((), (), s32[]{:S(2)}) async-start(), calls=%async_computation.8 | async-start | bytes 5242880 | tf_op jit(solution)/shard_map/reduce_scatter | solution.py:191
Sparse Core Ops, SparseCore 0:
  20.1 52.4 reduce-scatter.3
  641.0 72.9 reduce-scatter.7
  716.9 76.7 reduce-scatter.5
Sparse Core Ops, SparseCore 1:
  22.1 45.4 all-gather.10
  69.6 44.3 all-gather.4
  115.9 36.7 all-gather.6
  155.3 36.5 all-gather.8

commit v2 on v1

v2 whole, which is shorter than its diff:
```python
import functools

import jax
import jax.numpy as jnp
from jax import lax
from jax.experimental import pallas as pl
from jax.experimental.pallas import tpu as pltpu
from jax.sharding import PartitionSpec as P

NT = (((1,), (1,)), ((), ()))
BF16 = jnp.bfloat16
F32 = jnp.float32
MESH = pl.DeviceIdType.MESH
MIB = 1024 * 1024


def fit(size, want):
    while size % want:
        want //= 2
    return want


def to_row(column):
    return jnp.broadcast_to(column, (column.shape[0], 128)).T[:1]


def to_column(row):
    return jnp.broadcast_to(row, (128, row.shape[1])).T[:, :1]


def remote(src, dst, send, recv, device):
    return pltpu.make_async_remote_copy(
        src_ref=src, dst_ref=dst, send_sem=send, recv_sem=recv, device_id=device, device_id_type=MESH
    )


def greet(devices):
    barrier = pltpu.get_barrier_semaphore()
    for device in devices:
        pl.semaphore_signal(barrier, inc=1, device_id=device, device_id_type=MESH)
    pl.semaphore_wait(barrier, len(devices))


def row_peers(nrow):
    row, col = lax.axis_index("row"), lax.axis_index("col")
    half, pair, pairs = lax.rem(row, 2), row // 2, nrow // 2
    sibling = (pair * 2 + 1 - half, col)
    across = [(lax.rem(pair + d, pairs) * 2 + half, col) for d in range(1, pairs)]
    return row, half, pair, sibling, across


def gather_body(nrow, looked, back, tgt, tgt_all, w_all, pair_in, chip_in, own_w, *sems):
    (s1, r1, s2, r2, ts, tr, fs, fr, ws, wr, gs, gr, here) = sems
    pairs = nrow // 2
    row, half, pair, sibling, across = row_peers(nrow)
    greet([sibling] + across)

    first = [remote(looked.at[2 * q + 1 - half], pair_in.at[q], s1.at[q], r1.at[q], sibling) for q in range(pairs)]
    for copy in first:
        copy.start()
    keep = pltpu.make_async_copy(tgt, tgt_all.at[row], here.at[0])
    keep.start()
    tgt_out = [remote(tgt, tgt_all.at[row], ts.at[d], tr.at[d], to) for d, to in enumerate([sibling] + across)]
    for copy in tgt_out:
        copy.start()
    for copy in first:
        copy.wait()
    for q in range(pairs):
        pair_in[q] = (looked[2 * q + half].astype(F32) + pair_in[q].astype(F32)).astype(BF16)
    second = [
        remote(pair_in.at[lax.rem(pair + d, pairs)], chip_in.at[d], s2.at[d], r2.at[d], across[d - 1])
        for d in range(1, pairs)
    ]
    for copy in second:
        copy.start()
    for copy in second:
        copy.wait()
    looks = pair_in[pair].astype(F32)
    for d in range(1, pairs):
        looks = looks + chip_in[d].astype(F32)
    own_w[...] = (jnp.exp(looks) * back[...].astype(F32)).astype(BF16)
    keep_w = pltpu.make_async_copy(own_w, w_all.at[row], here.at[1])
    keep_w.start()
    w_out = [remote(own_w, w_all.at[row], ws.at[d], wr.at[d], to) for d, to in enumerate([sibling] + across)]
    for copy in w_out:
        copy.start()
    passed = []
    for out, whole, send, recv in ((tgt_out, tgt_all, fs, fr), (w_out, w_all, gs, gr)):
        for d in range(1, pairs):
            out[d].wait_recv()
            origin = lax.rem(pair - d + pairs, pairs) * 2 + half
            copy = remote(whole.at[origin], whole.at[origin], send.at[d], recv.at[d], sibling)
            copy.start()
            passed.append(copy)
        out[0].wait_recv()
        for copy in out:
            copy.wait_send()
    for copy in passed:
        copy.wait()
    keep.wait()
    keep_w.wait()


def gather_targets(nrow, looked, backward, tgt):
    seqs, cols = looked.shape
    part = seqs // nrow
    pairs = nrow // 2
    vmem = pl.BlockSpec(memory_space=pltpu.VMEM)
    hbm = pl.BlockSpec(memory_space=pl.ANY)
    dma = pltpu.SemaphoreType.DMA
    tgt_all, w_all = pl.pallas_call(
        functools.partial(gather_body, nrow),
        in_specs=[vmem, vmem, hbm],
        out_specs=[hbm, hbm],
        out_shape=[
            jax.ShapeDtypeStruct((nrow,) + tgt.shape, BF16),
            jax.ShapeDtypeStruct((nrow, part, cols), BF16),
        ],
        scratch_shapes=[
            pltpu.VMEM((pairs, part, cols), BF16),
            pltpu.VMEM((pairs, part, cols), BF16),
            pltpu.VMEM((part, cols), BF16),
        ]
        + [dma((pairs,))] * 12
        + [dma((2,))],
        compiler_params=pltpu.CompilerParams(
            collective_id=0, has_side_effects=True, vmem_limit_bytes=40 * MIB
        ),
        cost_estimate=pl.CostEstimate(flops=0, bytes_accessed=200 * MIB, transcendentals=0),
        name="gather_targets",
    )(looked.reshape(nrow, part, cols), backward, tgt)
    return tgt_all.reshape(nrow * tgt.shape[0], tgt.shape[1]), w_all.reshape(seqs, cols)


def first_pass(src, tgt, weighted):
    rows, width = src.shape
    cols = tgt.shape[0]
    seqs = weighted.shape[0]
    tile = fit(rows, 256)
    chunk = fit(cols, 2048)
    tiles = rows // tile

    def body(src_ref, tgt_ref, w_ref, e_ref, reach_ref, peak_ref, sum_ref, s0, s1, p0, p1):
        step = pl.program_id(0)

        def run(new, old, new_peak, old_peak):
            peak = old_peak[...]
            reach_ref[...] = jnp.zeros_like(reach_ref)

            def go(c, carry):
                best, total = carry
                at = pl.ds(pl.multiple_of(c * chunk, chunk), chunk)
                logits = lax.dot_general(src_ref[...], tgt_ref[at, :], NT, preferred_element_type=F32)
                new[:, at] = logits
                best = jnp.maximum(best, jnp.max(logits, axis=1, keepdims=True))
                e = jnp.exp(old[:, at] - peak)
                total = total + jnp.sum(e, axis=1, keepdims=True)
                eb = e.astype(BF16)
                e_ref[:, at] = eb
                reach_ref[...] += lax.dot_general(w_ref[:, at], eb, NT, preferred_element_type=F32)
                return best, total

            best, total = lax.fori_loop(
                0, cols // chunk, go, (jnp.full((tile, 1), -jnp.inf, F32), jnp.zeros((tile, 1), F32))
            )
            new_peak[...] = best
            sum_ref[...] = to_row(total)
            peak_ref[...] = to_row(peak)

        @pl.when(lax.rem(step, 2) == 0)
        def _():
            run(s0, s1, p0, p1)

        @pl.when(lax.rem(step, 2) == 1)
        def _():
            run(s1, s0, p1, p0)

    once = pl.Buffered(1)
    behind = lambda t: (jnp.maximum(t - 1, 0), 0)
    beside = lambda t: (0, jnp.maximum(t - 1, 0))
    whole = lambda t: (0, 0)
    return pl.pallas_call(
        body,
        grid=(tiles + 1,),
        in_specs=[
            pl.BlockSpec((tile, width), lambda t: (jnp.minimum(t, tiles - 1), 0)),
            pl.BlockSpec((cols, width), whole, pipeline_mode=once),
            pl.BlockSpec((seqs, cols), whole, pipeline_mode=once),
        ],
        out_specs=[
            pl.BlockSpec((tile, cols), behind),
            pl.BlockSpec((seqs, tile), beside),
            pl.BlockSpec((1, tile), beside),
            pl.BlockSpec((1, tile), beside),
        ],
        out_shape=[
            jax.ShapeDtypeStruct((rows, cols), BF16),
            jax.ShapeDtypeStruct((seqs, rows), F32),
            jax.ShapeDtypeStruct((1, rows), F32),
            jax.ShapeDtypeStruct((1, rows), F32),
        ],
        scratch_shapes=[
            pltpu.VMEM((tile, cols), F32),
            pltpu.VMEM((tile, cols), F32),
            pltpu.VMEM((tile, 1), F32),
            pltpu.VMEM((tile, 1), F32),
        ],
        compiler_params=pltpu.CompilerParams(
            dimension_semantics=("arbitrary",), vmem_limit_bytes=58 * MIB
        ),
        cost_estimate=pl.CostEstimate(
            flops=2 * rows * cols * (width + seqs), bytes_accessed=200 * MIB, transcendentals=rows * cols
        ),
        name="first_pass",
    )(src, tgt, weighted)


def weights_body(nrow, ncol, factor, chunk, peak, sums, reach, fwd, coeffs, share,
                 stats, terms_col, terms_row, counts, rate, *sems):
    (a_s, a_r, b_s, b_r, c_s, c_r, d_s, d_r) = sems
    row, col = lax.axis_index("row"), lax.axis_index("col")
    cols = [(row, lax.rem(col + d, ncol)) for d in range(1, ncol)]
    rows = [(lax.rem(row + d, nrow), col) for d in range(1, nrow)]
    greet(cols + rows)
    size = reach.shape[1]

    def share_out(buffer, send, recv, devices):
        copies = [
            remote(buffer.at[0], buffer.at[d + 1], send.at[d], recv.at[d], to) for d, to in enumerate(devices)
        ]
        for copy in copies:
            copy.start()
        for copy in copies:
            copy.wait()

    stats[0, 0:1, :] = peak[...]
    stats[0, 1:2, :] = sums[...]
    share_out(stats, a_s, a_r, cols)
    best = stats[0, 0:1, :]
    for d in range(1, ncol):
        best = jnp.maximum(best, stats[d, 0:1, :])
    total = jnp.zeros_like(best)
    for d in range(ncol):
        total = total + stats[d, 1:2, :] * jnp.exp(stats[d, 0:1, :] - best)
    rate[0:1, :] = jnp.exp(peak[...] - best) / total

    def norm(c, carry):
        at = pl.ds(pl.multiple_of(c * chunk, chunk), chunk)
        term = fwd[:, at].astype(F32) * reach[:, at] * rate[0:1, at]
        return carry + jnp.sum(term, axis=1, keepdims=True)

    seqs = reach.shape[0]
    terms = lax.fori_loop(0, size // chunk, norm, jnp.zeros((seqs, 1), F32))
    terms_col[0] = to_row(terms)
    share_out(terms_col, b_s, b_r, cols)
    part = terms_col[0]
    for d in range(1, ncol):
        part = part + terms_col[d]
    terms_row[0] = part
    share_out(terms_row, c_s, c_r, rows)
    part = terms_row[0]
    for d in range(1, nrow):
        part = part + terms_row[d]
    inverse = to_column(factor / part)

    def weigh(c, carry):
        at = pl.ds(pl.multiple_of(c * chunk, chunk), chunk)
        made = (fwd[:, at].astype(F32) * inverse * rate[0:1, at]).astype(BF16)
        coeffs[:, at] = made
        counts[0, :, at] = jnp.sum(made.astype(F32) * reach[:, at], axis=0, keepdims=True)
        return carry

    lax.fori_loop(0, size // chunk, weigh, 0)
    share_out(counts, d_s, d_r, cols)
    count = counts[0]
    for d in range(1, ncol):
        count = count + counts[d]
    share[...] = count * rate[0:1, :]


def make_weights(nrow, ncol, factor, peak, sums, reach, forward):
    seqs, rows = reach.shape
    vmem = pl.BlockSpec(memory_space=pltpu.VMEM)
    dma = pltpu.SemaphoreType.DMA
    return pl.pallas_call(
        functools.partial(weights_body, nrow, ncol, factor, fit(rows, 512)),
        in_specs=[vmem] * 4,
        out_specs=[vmem] * 2,
        out_shape=[jax.ShapeDtypeStruct((seqs, rows), BF16), jax.ShapeDtypeStruct((1, rows), F32)],
        scratch_shapes=[
            pltpu.VMEM((ncol, 2, rows), F32),
            pltpu.VMEM((ncol, 1, seqs), F32),
            pltpu.VMEM((nrow, 1, seqs), F32),
            pltpu.VMEM((ncol, 1, rows), F32),
            pltpu.VMEM((1, rows), F32),
        ]
        + [dma((ncol - 1,))] * 4
        + [dma((nrow - 1,))] * 2
        + [dma((ncol - 1,))] * 2,
        compiler_params=pltpu.CompilerParams(
            collective_id=1, has_side_effects=True, vmem_limit_bytes=40 * MIB
        ),
        cost_estimate=pl.CostEstimate(flops=0, bytes_accessed=30 * MIB, transcendentals=0),
        name="make_weights",
    )(peak, sums, reach, forward)


def second_pass(exp_block, coeffs, share, weighted, tgt, src):
    rows, cols = exp_block.shape
    width = tgt.shape[1]
    seqs = weighted.shape[0]
    tile = fit(rows, 512)
    chunk = fit(cols, 512)
    group = 4 if (cols // chunk) % 4 == 0 else 1
    tiles = rows // tile
    turn = fit(cols, 1024)

    def body(e_ref, c_ref, share_ref, w_ref, tgt_ref, src_ref, gs_ref, gt_ref, total_ref):
        step = pl.program_id(0)

        @pl.when(step == 0)
        def _():
            total_ref[...] = jnp.zeros_like(total_ref)

        lead = c_ref[...].astype(F32).T.astype(BF16)
        flipped = src_ref[...].astype(F32).T.astype(BF16)
        level = to_column(share_ref[...])

        def go(c, total):
            for k in range(group):
                at = pl.ds(pl.multiple_of((c * group + k) * chunk, chunk), chunk)
                summed = jnp.dot(lead, w_ref[:, at], preferred_element_type=F32)
                g = (e_ref[:, at].astype(F32) * (summed - level)).astype(BF16)
                total = total + jnp.dot(g, tgt_ref[at, :], preferred_element_type=F32)
                total_ref[:, at] += jnp.dot(flipped, g, preferred_element_type=F32)
            return total

        made = lax.fori_loop(0, cols // chunk // group, go, jnp.zeros((tile, width), F32))
        gs_ref[...] = made.astype(BF16)

        @pl.when(step == tiles - 1)
        def _():
            def flip(c, carry):
                at = pl.ds(pl.multiple_of(c * turn, turn), turn)
                gt_ref[at, :] = total_ref[:, at].T.astype(BF16)
                return carry

            lax.fori_loop(0, cols // turn, flip, 0)

    once = pl.Buffered(1)
    by_row = lambda t: (t, 0)
    beside = lambda t: (0, t)
    whole = lambda t: (0, 0)
    return pl.pallas_call(
        body,
        grid=(tiles,),
        in_specs=[
            pl.BlockSpec((tile, cols), by_row),
            pl.BlockSpec((seqs, tile), beside),
            pl.BlockSpec((1, tile), beside),
            pl.BlockSpec((seqs, cols), whole, pipeline_mode=once),
            pl.BlockSpec((cols, width), whole, pipeline_mode=once),
            pl.BlockSpec((tile, width), by_row),
        ],
        out_specs=[
            pl.BlockSpec((tile, width), by_row),
            pl.BlockSpec((cols, width), whole, pipeline_mode=once),
        ],
        out_shape=[
            jax.ShapeDtypeStruct((rows, width), BF16),
            jax.ShapeDtypeStruct((cols, width), BF16),
        ],
        scratch_shapes=[pltpu.VMEM((width, cols), F32)],
        compiler_params=pltpu.CompilerParams(
            dimension_semantics=("arbitrary",), vmem_limit_bytes=58 * MIB
        ),
        cost_estimate=pl.CostEstimate(
            flops=2 * rows * cols * (2 * width + seqs), bytes_accessed=100 * MIB, transcendentals=0
        ),
        name="second_pass",
    )(exp_block, coeffs, share, weighted, tgt, src)


def scatter_body(nrow, ncol, ps, pt, out_src, out_tgt, col_in, pair_in, pair_out, chip_in, *sems):
    (a_s, a_r, b_s, b_r, c_s, c_r) = sems
    pairs = nrow // 2
    row, half, pair, sibling, across = row_peers(nrow)
    col = lax.axis_index("col")
    places = [lax.rem(col + d, ncol) for d in range(1, ncol)]
    greet([sibling] + across + [(row, place) for place in places])
    first = [remote(pt.at[2 * q + 1 - half], pair_in.at[q], b_s.at[q], b_r.at[q], sibling) for q in range(pairs)]
    for copy in first:
        copy.start()
    along = [
        remote(ps.at[place], col_in.at[d], a_s.at[d], a_r.at[d], (row, place)) for d, place in enumerate(places)
    ]
    for copy in along:
        copy.start()
    for copy in first:
        copy.wait()
    for d in range(1, pairs):
        q = lax.rem(pair + d, pairs)
        pair_out[d] = (pt[2 * q + half].astype(F32) + pair_in[q].astype(F32)).astype(BF16)
    second = [remote(pair_out.at[d], chip_in.at[d], c_s.at[d], c_r.at[d], across[d - 1]) for d in range(1, pairs)]
    for copy in second:
        copy.start()
    total = pt[2 * pair + half].astype(F32) + pair_in[pair].astype(F32)
    for d, copy in enumerate(second):
        copy.wait()
        total = total + chip_in[d + 1].astype(F32)
    out_tgt[...] = total
    total = ps[col].astype(F32)
    for d, copy in enumerate(along):
        copy.wait()
        total = total + col_in[d].astype(F32)
    out_src[...] = total


def scatter_sums(nrow, ncol, part_src, part_tgt):
    width = part_src.shape[1]
    src_rows = part_src.shape[0] // ncol
    tgt_rows = part_tgt.shape[0] // nrow
    pairs = nrow // 2
    vmem = pl.BlockSpec(memory_space=pltpu.VMEM)
    dma = pltpu.SemaphoreType.DMA
    return pl.pallas_call(
        functools.partial(scatter_body, nrow, ncol),
        in_specs=[vmem] * 2,
        out_specs=[vmem] * 2,
        out_shape=[
            jax.ShapeDtypeStruct((src_rows, width), F32),
            jax.ShapeDtypeStruct((tgt_rows, width), F32),
        ],
        scratch_shapes=[
            pltpu.VMEM((ncol - 1, src_rows, width), BF16),
            pltpu.VMEM((pairs, tgt_rows, width), BF16),
            pltpu.VMEM((pairs, tgt_rows, width), BF16),
            pltpu.VMEM((pairs, tgt_rows, width), BF16),
        ]
        + [dma((ncol - 1,))] * 2
        + [dma((pairs,))] * 4,
        compiler_params=pltpu.CompilerParams(
            collective_id=2, has_side_effects=True, vmem_limit_bytes=40 * MIB
        ),
        cost_estimate=pl.CostEstimate(flops=0, bytes_accessed=100 * MIB, transcendentals=0),
        name="scatter_sums",
    )(part_src.reshape(ncol, src_rows, width), part_tgt.reshape(nrow, tgt_rows, width))


def on_device(nrow, ncol, tokens, emission_table, forward_rows, backward_rows, src_embed, tgt_embed):
    src_block = lax.all_gather(src_embed, "col", axis=0, tiled=True)
    forward_all = lax.all_gather(forward_rows, "col", axis=0, tiled=True)
    vocab_local = emission_table.shape[0]
    offset = lax.axis_index("row") * vocab_local
    onehot = (tokens[:, None] == offset + jnp.arange(vocab_local, dtype=jnp.int32)[None, :]).astype(BF16)
    looked = jnp.dot(onehot, emission_table, preferred_element_type=F32).astype(BF16)
    tgt_block, weighted = gather_targets(nrow, looked, backward_rows, tgt_embed)
    exp_block, reach, peak, sums = first_pass(src_block, tgt_block, weighted)
    factor = forward_rows.shape[1] * nrow / tokens.shape[0]
    coeffs, share = make_weights(nrow, ncol, factor, peak, sums, reach, forward_all)
    part_src, part_tgt = second_pass(exp_block, coeffs, share, weighted, tgt_block, src_block)
    return scatter_sums(nrow, ncol, part_src, part_tgt)


def solution(mesh):
    in_specs = (
        P(),
        P("row", "col"),
        P("col", "row"),
        P("row", "col"),
        P(("row", "col"), None),
        P(("col", "row"), None),
    )
    out_specs = (P(("row", "col"), None), P(("col", "row"), None))
    return jax.shard_map(
        functools.partial(on_device, mesh.shape["row"], mesh.shape["col"]),
        mesh=mesh,
        in_specs=in_specs,
        out_specs=out_specs,
        check_vma=False,
    )
```

time: 803 us -> 344 us (0.43)
  waiting for transfers between devices: 311 us -> 1.39 us
  blocking collectives: 263 us -> 0 us
  Pallas kernels: 163 us -> 301 us
  other arithmetic: 22.2 us -> 0.01 us
    reduce_scatter x3 -> x0, waiting for transfers between devices: 199 us -> none  [the longest x1 77.1 us: on_device(): lax.psum_scatter(part_src, 'col', scatter_dimension=0, tiled=True)]
    psum x3 -> x0, blocking collectives: 188 us -> none  [the longest x1 74.6 us: on_device(): row_sums = lax.psum(local_sums * scale, 'col')]
    pallas_call x1 -> x4, Pallas kernels: 71.9 us -> 220 us  [the longest x1 76.3 us: gather_targets(): pl.pallas_call(functools.partial(gather_body, nrow), in_specs=[vmem, vmem...]
    pmax x1 -> x0, blocking collectives: 75.5 us -> none  [on_device(): row_peak = lax.pmax(local_peak, 'col')]
    all_gather x3 -> x1, waiting for transfers between devices: 73.8 us -> 0.02 us  [on_device(): forward_all = lax.all_gather(forward_rows, 'col', axis=0, tiled=True)]
    all_gather x1, waiting for transfers between devices: 35.9 us -> 0.01 us  [on_device(): src_block = lax.all_gather(src_embed, 'col', axis=0, tiled=True)]
    unnamed x8 -> x26, local copies, waits for them, and re-layouts: 3.92 us -> 16.8 us
    pallas_call x1, Pallas kernels: 91.4 us -> 80.3 us  [first_pass(): pl.pallas_call(body, grid=(tiles + 1,), in_specs=[pl.BlockSpec((tile, wid...]
  transfers between devices with their start and end apart: 7 -> 2, of which waited for: 6 -> 0; matrix products, arithmetic and copies ran while one was open for 2% -> 3% of each run, Pallas kernels for 0% -> 46%
where the time goes in v2:
time: 344 us
  Pallas kernels  301 us (88%)
  local copies, waits for them, and re-layouts  16.8 us (5%)
  between operations  14.2 us (4%)
  matrix products  10.7 us (3%)
    pallas_call x1, Pallas kernels, first_pass(): pl.pallas_call(body, grid=(tiles + 1,), in_specs=[pl.BlockSpec((tile, wid...  80.3 us
    pallas_call x1, Pallas kernels, gather_targets(): pl.pallas_call(functools.partial(gather_body, nrow), in_specs=[vmem, vmem...  76.3 us
    pallas_call x1, Pallas kernels, second_pass(): pl.pallas_call(body, grid=(tiles,), in_specs=[pl.BlockSpec((tile, cols),...  75.3 us
    pallas_call x1, Pallas kernels, scatter_sums(): pl.pallas_call(functools.partial(scatter_body, nrow, ncol), in_specs=[vme...  48.7 us
    pallas_call x1, Pallas kernels, make_weights(): pl.pallas_call(functools.partial(weights_body, nrow, ncol, factor, fit(ro...  20 us
    unnamed x26, local copies, waits for them, and re-layouts  16.8 us
    dot_general x1, matrix products, on_device(): jnp.dot(onehot, emission_table, preferred_element_type=F32).astype(BF16)  10.7 us
  transfers between devices with their start and end apart: 2, of which 0 were waited for; matrix products, arithmetic and copies ran while one was open for 3% of the time, Pallas kernels for 46%

profile of v2, /device:TPU:8, one launch (start us, length us, event | category | flops | bytes accessed | tf_op | source)
XLA Modules:
  0.0 343.7 jit_solution(7012927678038825087)
XLA Ops:
  7.2 0.0 all-gather.3.cloned.1.call-start
  7.2 0.7 all-gather.3.cloned.1.call-update
  7.9 0.0 all-gather.5.cloned.1.call-start
  7.9 0.7 all-gather.5.cloned.1.call-update
  8.7 0.0 copy-start.4
  8.7 0.0 copy-start.5
  8.7 10.7 %convolution_convert_fusion = bf16[256,8192]{1,0:T(8,128)(2,1)S(1)} fusion(bf16[1024,8192]{1,0:T(8,128)(2,1)} %param.7, s32[1024]{0:T(1024)S(1)} %iota_add_fusion, s32[256]{0:T(256)} %param.6), kind=kOutput, calls=%fused_computation | convolution fusion | flops 4297326592 | bytes 20976640 | tf_op jit(solution)/shard_map/dot_general | solution.py:456
  19.4 0.0 copy-done.4
  19.4 0.0 copy-done.5
  19.4 76.3 %gather_targets.1 = (bf16[8,1024,256]{2,1,0:T(8,128)(2,1)S(1)}, bf16[8,32,8192]{2,1,0:T(8,128)(2,1)S(1)}) custom-call(bf16[8,32,8192]{2,1,0:T(8,128)(2,1)S(1)} %bitcast.6, bf16[32,8192]{1,0:T(8,128)(2,1)S(1)} %copy-done.4, bf16[1024,256]{1,0:T(8,128)(2,1)S(1)} %copy-done.5), custom_call_target="tpu_custom_call" | custom-call | bytes 209715200 | tf_op jit(solution)/shard_map/gather_targets/pallas_call | solution.py:111
  95.7 0.0 copy-start.8
  95.8 2.0 copy-done.8
  97.7 0.0 copy-start.9
  97.7 2.0 copy-done.9
  99.7 0.0 all-gather.3.cloned.1.call-done.src_ref
  99.7 80.3 %first_pass.1 = (bf16[4096,8192]{1,0:T(8,128)(2,1)}, f32[256,4096]{1,0:T(8,128)}, f32[1,4096]{1,0:T(1,128)}, f32[1,4096]{1,0:T(1,128)}) custom-call(bf16[4096,256]{1,0:T(8,128)(2,1)} %all-gather.3.cloned.1.call-done.src_ref, bf16[8192,256]{1,0:T(8,128)(2,1)} %bitcast.9, bf16[256,8192]{1,0:T(8,128)(2,1)} %bitcast.11), custom_call_target="tpu_custom_call" | custom-call | flops 34359738368 | bytes 209715200 | tf_op jit(solution)/shard_map/first_pass/pallas_call | solution.py:182
  180.0 0.0 all-gather.5.cloned.1.call-done.fwd
  180.0 0.0 copy-start
  180.1 2.2 copy-done
  182.2 1.6 copy-done.2
  183.8 0.7 copy-done.6
  184.5 0.7 copy-done.7
  185.3 20.0 %make_weights.1 = (bf16[256,4096]{1,0:T(8,128)(2,1)S(1)}, f32[1,4096]{1,0:T(1,128)S(1)}) custom-call(f32[1,4096]{1,0:T(1,128)S(1)} %copy-done.6, f32[1,4096]{1,0:T(1,128)S(1)} %copy-done.7, f32[256,4096]{1,0:T(8,128)S(1)} %copy-done, bf16[256,4096]{1,0:T(8,128)(2,1)S(1)} %copy-done.2), custom_call_target="tpu_custom_call" | custom-call | bytes 31457280 | tf_op jit(solution)/shard_map/make_weights/pallas_call | solution.py:285
  205.3 0.0 copy-start.10
  205.3 1.3 copy-done.10
  206.6 0.6 copy-done.11
  207.2 75.3 %second_pass.1 = (bf16[4096,256]{1,0:T(8,128)(2,1)}, bf16[8192,256]{1,0:T(8,128)(2,1)}) custom-call(bf16[4096,8192]{1,0:T(8,128)(2,1)} %get-tuple-element.14.e_ref, bf16[256,4096]{1,0:T(8,128)(2,1)} %copy-done.10, f32[1,4096]{1,0:T(1,128)} %copy-done.11, bf16[256,8192]{1,0:T(8,128)(2,1)} %bitcast.12, bf16[8192,256]{1,0:T(8,128)(2,1)} %bitcast.10, ...), custom_call_target="tpu_custom_call" | custom-call | flops 51539607552 | bytes 104857600 | tf_op jit(solution)/shard_map/second_pass/pallas_call | solution.py:354
  282.5 2.2 copy-done.1
  284.7 1.6 copy-done.3
  286.2 48.7 %scatter_sums.1 = (f32[1024,256]{1,0:T(8,128)S(1)}, f32[1024,256]{1,0:T(8,128)S(1)}) custom-call(bf16[4,1024,256]{2,1,0:T(8,128)(2,1)S(1)} %bitcast.8, bf16[8,1024,256]{2,1,0:T(8,128)(2,1)S(1)} %bitcast.7), custom_call_target="tpu_custom_call" | custom-call | bytes 104857600 | tf_op jit(solution)/shard_map/scatter_sums/pallas_call | solution.py:426
  335.0 1.0 copy.10
  335.9 1.0 copy.11
  (7 shorter events, 0.0 us)
Async XLA Ops:
  7.2 92.5 %all-gather.3.cloned.1.call-start = ((), (), s32[]{:S(2)}) async-start(), calls=%async_computation | async-start | bytes 2621440 | tf_op jit(solution)/shard_map/all_gather | solution.py:451
  7.9 172.1 %all-gather.5.cloned.1.call-start = ((), (), s32[]{:S(2)}) async-start(), calls=%async_computation.1 | async-start | bytes 2621440 | tf_op jit(solution)/shard_map/all_gather | solution.py:452
  8.7 10.7 %copy-start.4 = (bf16[32,8192]{1,0:T(8,128)(2,1)S(1)}, bf16[32,8192]{1,0:T(8,128)(2,1)}, u32[]{:S(2)}) copy-start(bf16[32,8192]{1,0:T(8,128)(2,1)} %back.1) | copy-start | bytes 1572868
  8.7 10.7 %copy-start.5 = (bf16[1024,256]{1,0:T(8,128)(2,1)S(1)}, bf16[1024,256]{1,0:T(8,128)(2,1)}, u32[]{:S(2)}) copy-start(bf16[1024,256]{1,0:T(8,128)(2,1)} %tgt.1) | copy-start | bytes 1572868
  95.7 2.0 copy-start.8
  97.7 2.0 copy-start.9
  180.0 2.2 copy-start
  182.2 1.6 copy-start.2
  183.8 0.7 copy-start.6
  184.5 0.7 copy-start.7
  205.3 1.3 copy-start.10
  206.6 0.6 copy-start.11
  282.5 2.2 copy-start.1
  284.6 1.6 copy-start.3
Sparse Core Ops, SparseCore 0:
  9.6 45.4 all-gather.2
  56.7 44.9 all-gather.4

commit v3 on v2

--- a/solution.py
+++ b/solution.py
@@ -49,170 +49,225 @@
     return row, half, pair, sibling, across
 
 
-def gather_body(nrow, looked, back, tgt, tgt_all, w_all, pair_in, chip_in, own_w, *sems):
-    (s1, r1, s2, r2, ts, tr, fs, fr, ws, wr, gs, gr, here) = sems
+def gather_body(nrow, looked, tgt, tgt_all, pair_sum, pair_in, *sems):
+    (s1, r1, ts, tr, fs, fr, here) = sems
     pairs = nrow // 2
     row, half, pair, sibling, across = row_peers(nrow)
     greet([sibling] + across)
 
+    tgt_out = [remote(tgt, tgt_all.at[row], ts.at[d], tr.at[d], to) for d, to in enumerate([sibling] + across)]
+    for copy in tgt_out:
+        copy.start()
+    keep = pltpu.make_async_copy(tgt, tgt_all.at[row], here)
+    keep.start()
     first = [remote(looked.at[2 * q + 1 - half], pair_in.at[q], s1.at[q], r1.at[q], sibling) for q in range(pairs)]
     for copy in first:
         copy.start()
-    keep = pltpu.make_async_copy(tgt, tgt_all.at[row], here.at[0])
-    keep.start()
-    tgt_out = [remote(tgt, tgt_all.at[row], ts.at[d], tr.at[d], to) for d, to in enumerate([sibling] + across)]
+    for q, copy in enumerate(first):
+        copy.wait()
+        pair_sum[q] = (looked[2 * q + half].astype(F32) + pair_in[q].astype(F32)).astype(BF16)
+    passed = []
+    for d in range(1, pairs):
+        tgt_out[d].wait_recv()
+        origin = lax.rem(pair - d + pairs, pairs) * 2 + half
+        copy = remote(tgt_all.at[origin], tgt_all.at[origin], fs.at[d], fr.at[d], sibling)
+        copy.start()
+        passed.append(copy)
+    tgt_out[0].wait_recv()
     for copy in tgt_out:
-        copy.start()
-    for copy in first:
-        copy.wait()
-    for q in range(pairs):
-        pair_in[q] = (looked[2 * q + half].astype(F32) + pair_in[q].astype(F32)).astype(BF16)
-    second = [
-        remote(pair_in.at[lax.rem(pair + d, pairs)], chip_in.at[d], s2.at[d], r2.at[d], across[d - 1])
-        for d in range(1, pairs)
-    ]
-    for copy in second:
-        copy.start()
-    for copy in second:
-        copy.wait()
-    looks = pair_in[pair].astype(F32)
-    for d in range(1, pairs):
-        looks = looks + chip_in[d].astype(F32)
-    own_w[...] = (jnp.exp(looks) * back[...].astype(F32)).astype(BF16)
-    keep_w = pltpu.make_async_copy(own_w, w_all.at[row], here.at[1])
-    keep_w.start()
-    w_out = [remote(own_w, w_all.at[row], ws.at[d], wr.at[d], to) for d, to in enumerate([sibling] + across)]
-    for copy in w_out:
-        copy.start()
-    passed = []
-    for out, whole, send, recv in ((tgt_out, tgt_all, fs, fr), (w_out, w_all, gs, gr)):
-        for d in range(1, pairs):
-            out[d].wait_recv()
-            origin = lax.rem(pair - d + pairs, pairs) * 2 + half
-            copy = remote(whole.at[origin], whole.at[origin], send.at[d], recv.at[d], sibling)
-            copy.start()
-            passed.append(copy)
-        out[0].wait_recv()
-        for copy in out:
-            copy.wait_send()
+        copy.wait_send()
     for copy in passed:
         copy.wait()
     keep.wait()
-    keep_w.wait()
-
-
-def gather_targets(nrow, looked, backward, tgt):
+
+
+def gather_targets(nrow, looked, tgt):
     seqs, cols = looked.shape
     part = seqs // nrow
     pairs = nrow // 2
     vmem = pl.BlockSpec(memory_space=pltpu.VMEM)
     hbm = pl.BlockSpec(memory_space=pl.ANY)
     dma = pltpu.SemaphoreType.DMA
-    tgt_all, w_all = pl.pallas_call(
+    tgt_all, pair_sum = pl.pallas_call(
         functools.partial(gather_body, nrow),
-        in_specs=[vmem, vmem, hbm],
-        out_specs=[hbm, hbm],
+        in_specs=[vmem, hbm],
+        out_specs=[hbm, vmem],
         out_shape=[
             jax.ShapeDtypeStruct((nrow,) + tgt.shape, BF16),
-            jax.ShapeDtypeStruct((nrow, part, cols), BF16),
-        ],
-        scratch_shapes=[
-            pltpu.VMEM((pairs, part, cols), BF16),
-            pltpu.VMEM((pairs, part, cols), BF16),
-            pltpu.VMEM((part, cols), BF16),
-        ]
-        + [dma((pairs,))] * 12
-        + [dma((2,))],
+            jax.ShapeDtypeStruct((pairs, part, cols), BF16),
+        ],
+        scratch_shapes=[pltpu.VMEM((pairs, part, cols), BF16)] + [dma((pairs,))] * 6 + [dma],
         compiler_params=pltpu.CompilerParams(
             collective_id=0, has_side_effects=True, vmem_limit_bytes=40 * MIB
         ),
-        cost_estimate=pl.CostEstimate(flops=0, bytes_accessed=200 * MIB, transcendentals=0),
+        cost_estimate=pl.CostEstimate(flops=0, bytes_accessed=100 * MIB, transcendentals=0),
         name="gather_targets",
-    )(looked.reshape(nrow, part, cols), backward, tgt)
-    return tgt_all.reshape(nrow * tgt.shape[0], tgt.shape[1]), w_all.reshape(seqs, cols)
-
-
-def first_pass(src, tgt, weighted):
+    )(looked.reshape(nrow, part, cols), tgt)
+    return tgt_all.reshape(nrow * tgt.shape[0], tgt.shape[1]), pair_sum
+
+
+def exp_body(nrow, tiles, chunk, src_ref, tgt_ref, pair_sum, back, e_ref, peak_ref, sum_ref, w_all,
+             s0, s1, p0, p1, chip_in, own_w, *sems):
+    (s2, r2, ws, wr, gs, gr, here) = sems
+    pairs = nrow // 2
+    row, half, pair, sibling, across = row_peers(nrow)
+    step = pl.program_id(0)
+    tile, cols = e_ref.shape
+
+    second = [
+        remote(pair_sum.at[lax.rem(pair + d, pairs)], chip_in.at[d], s2.at[d], r2.at[d], across[d - 1])
+        for d in range(1, pairs)
+    ]
+    keep = pltpu.make_async_copy(own_w, w_all.at[row], here)
+    out = [remote(own_w, w_all.at[row], ws.at[d], wr.at[d], to) for d, to in enumerate([sibling] + across)]
+    passed = []
+    for d in range(1, pairs):
+        origin = lax.rem(pair - d + pairs, pairs) * 2 + half
+        passed.append(remote(w_all.at[origin], w_all.at[origin], gs.at[d], gr.at[d], sibling))
+
+    @pl.when(step == 0)
+    def _():
+        greet([sibling] + across)
+        for copy in second:
+            copy.start()
+
+    @pl.when(step == max(tiles // 2 - 1, 0))
+    def _():
+        looks = pair_sum[pair].astype(F32)
+        for d, copy in enumerate(second):
+            copy.wait()
+            looks = looks + chip_in[d + 1].astype(F32)
+        own_w[...] = (jnp.exp(looks) * back[...].astype(F32)).astype(BF16)
+        for copy in out:
+            copy.start()
+        keep.start()
+
+    @pl.when(step == tiles - 1)
+    def _():
+        for copy, along in zip(out[1:], passed):
+            copy.wait_recv()
+            along.start()
+
+    def run(new, old, new_peak, old_peak):
+        peak = old_peak[...]
+
+        def go(c, carry):
+            best, total = carry
+            at = pl.ds(pl.multiple_of(c * chunk, chunk), chunk)
+            logits = lax.dot_general(src_ref[...], tgt_ref[at, :], NT, preferred_element_type=F32)
+            new[:, at] = logits
+            best = jnp.maximum(best, jnp.max(logits, axis=1, keepdims=True))
+            e = jnp.exp(old[:, at] - peak)
+            e_ref[:, at] = e.astype(BF16)
+            return best, total + jnp.sum(e, axis=1, keepdims=True)
+
+        best, total = lax.fori_loop(
+            0, cols // chunk, go, (jnp.full((tile, 1), -jnp.inf, F32), jnp.zeros((tile, 1), F32))
+        )
+        new_peak[...] = best
+        sum_ref[...] = to_row(total)
+        peak_ref[...] = to_row(peak)
+
+    @pl.when(lax.rem(step, 2) == 0)
+    def _():
+        run(s0, s1, p0, p1)
+
+    @pl.when(lax.rem(step, 2) == 1)
+    def _():
+        run(s1, s0, p1, p0)
+
+    @pl.when(step == tiles)
+    def _():
+        out[0].wait_recv()
+        for copy in out:
+            copy.wait_send()
+        for copy in passed:
+            copy.wait()
+        keep.wait()
+
+
+def exp_pass(nrow, src, tgt, pair_sum, backward):
     rows, width = src.shape
     cols = tgt.shape[0]
-    seqs = weighted.shape[0]
+    pairs, part = pair_sum.shape[:2]
     tile = fit(rows, 256)
     chunk = fit(cols, 2048)
     tiles = rows // tile
-
-    def body(src_ref, tgt_ref, w_ref, e_ref, reach_ref, peak_ref, sum_ref, s0, s1, p0, p1):
-        step = pl.program_id(0)
-
-        def run(new, old, new_peak, old_peak):
-            peak = old_peak[...]
-            reach_ref[...] = jnp.zeros_like(reach_ref)
-
-            def go(c, carry):
-                best, total = carry
-                at = pl.ds(pl.multiple_of(c * chunk, chunk), chunk)
-                logits = lax.dot_general(src_ref[...], tgt_ref[at, :], NT, preferred_element_type=F32)
-                new[:, at] = logits
-                best = jnp.maximum(best, jnp.max(logits, axis=1, keepdims=True))
-                e = jnp.exp(old[:, at] - peak)
-                total = total + jnp.sum(e, axis=1, keepdims=True)
-                eb = e.astype(BF16)
-                e_ref[:, at] = eb
-                reach_ref[...] += lax.dot_general(w_ref[:, at], eb, NT, preferred_element_type=F32)
-                return best, total
-
-            best, total = lax.fori_loop(
-                0, cols // chunk, go, (jnp.full((tile, 1), -jnp.inf, F32), jnp.zeros((tile, 1), F32))
-            )
-            new_peak[...] = best
-            sum_ref[...] = to_row(total)
-            peak_ref[...] = to_row(peak)
-
-        @pl.when(lax.rem(step, 2) == 0)
-        def _():
-            run(s0, s1, p0, p1)
-
-        @pl.when(lax.rem(step, 2) == 1)
-        def _():
-            run(s1, s0, p1, p0)
-
     once = pl.Buffered(1)
     behind = lambda t: (jnp.maximum(t - 1, 0), 0)
     beside = lambda t: (0, jnp.maximum(t - 1, 0))
     whole = lambda t: (0, 0)
-    return pl.pallas_call(
-        body,
+    dma = pltpu.SemaphoreType.DMA
+    exp_block, peak, sums, w_all = pl.pallas_call(
+        functools.partial(exp_body, nrow, tiles, chunk),
         grid=(tiles + 1,),
         in_specs=[
             pl.BlockSpec((tile, width), lambda t: (jnp.minimum(t, tiles - 1), 0)),
             pl.BlockSpec((cols, width), whole, pipeline_mode=once),
-            pl.BlockSpec((seqs, cols), whole, pipeline_mode=once),
+            pl.BlockSpec(pair_sum.shape, lambda t: (0, 0, 0), pipeline_mode=once),
+            pl.BlockSpec(backward.shape, whole, pipeline_mode=once),
         ],
         out_specs=[
             pl.BlockSpec((tile, cols), behind),
-            pl.BlockSpec((seqs, tile), beside),
             pl.BlockSpec((1, tile), beside),
             pl.BlockSpec((1, tile), beside),
+            pl.BlockSpec(memory_space=pl.ANY),
         ],
         out_shape=[
             jax.ShapeDtypeStruct((rows, cols), BF16),
-            jax.ShapeDtypeStruct((seqs, rows), F32),
             jax.ShapeDtypeStruct((1, rows), F32),
             jax.ShapeDtypeStruct((1, rows), F32),
+            jax.ShapeDtypeStruct((nrow, part, cols), BF16),
         ],
         scratch_shapes=[
             pltpu.VMEM((tile, cols), F32),
             pltpu.VMEM((tile, cols), F32),
             pltpu.VMEM((tile, 1), F32),
             pltpu.VMEM((tile, 1), F32),
-        ],
+            pltpu.VMEM((pairs, part, cols), BF16),
+            pltpu.VMEM((part, cols), BF16),
+        ]
+        + [dma((pairs,))] * 6
+        + [dma],
+        compiler_params=pltpu.CompilerParams(
+            dimension_semantics=("arbitrary",), collective_id=3, has_side_effects=True, vmem_limit_bytes=58 * MIB
+        ),
+        cost_estimate=pl.CostEstimate(
+            flops=2 * rows * cols * width, bytes_accessed=200 * MIB, transcendentals=rows * cols
+        ),
+        name="exp_pass",
+    )(src, tgt, pair_sum, backward)
+    return exp_block, peak, sums, w_all.reshape(nrow * part, cols)
+
+
+def reach_pass(exp_block, weighted):
+    rows, cols = exp_block.shape
+    seqs = weighted.shape[0]
+    tile = fit(rows, 512)
+    chunk = fit(cols, 2048)
+
+    def body(w_ref, e_ref, reach_ref):
+        total = jnp.zeros(reach_ref.shape, F32)
+        for c in range(cols // chunk):
+            at = pl.ds(c * chunk, chunk)
+            total = total + lax.dot_general(w_ref[:, at], e_ref[:, at], NT, preferred_element_type=F32)
+        reach_ref[...] = total
+
+    return pl.pallas_call(
+        body,
+        grid=(rows // tile,),
+        in_specs=[
+            pl.BlockSpec((seqs, cols), lambda t: (0, 0), pipeline_mode=pl.Buffered(1)),
+            pl.BlockSpec((tile, cols), lambda t: (t, 0)),
+        ],
+        out_specs=pl.BlockSpec((seqs, tile), lambda t: (0, t)),
+        out_shape=jax.ShapeDtypeStruct((seqs, rows), F32),
         compiler_params=pltpu.CompilerParams(
             dimension_semantics=("arbitrary",), vmem_limit_bytes=58 * MIB
         ),
-        cost_estimate=pl.CostEstimate(
-            flops=2 * rows * cols * (width + seqs), bytes_accessed=200 * MIB, transcendentals=rows * cols
-        ),
-        name="first_pass",
-    )(src, tgt, weighted)
+        cost_estimate=pl.CostEstimate(flops=2 * rows * cols * seqs, bytes_accessed=2 * rows * cols, transcendentals=0),
+        name="reach_pass",
+    )(weighted, exp_block)
 
 
 def weights_body(nrow, ncol, factor, chunk, peak, sums, reach, fwd, coeffs, share,
@@ -310,8 +365,7 @@
     width = tgt.shape[1]
     seqs = weighted.shape[0]
     tile = fit(rows, 512)
-    chunk = fit(cols, 512)
-    group = 4 if (cols // chunk) % 4 == 0 else 1
+    chunk = fit(cols, 1024)
     tiles = rows // tile
     turn = fit(cols, 1024)
 
@@ -326,16 +380,20 @@
         flipped = src_ref[...].astype(F32).T.astype(BF16)
         level = to_column(share_ref[...])
 
-        def go(c, total):
-            for k in range(group):
-                at = pl.ds(pl.multiple_of((c * group + k) * chunk, chunk), chunk)
-                summed = jnp.dot(lead, w_ref[:, at], preferred_element_type=F32)
-                g = (e_ref[:, at].astype(F32) * (summed - level)).astype(BF16)
-                total = total + jnp.dot(g, tgt_ref[at, :], preferred_element_type=F32)
-                total_ref[:, at] += jnp.dot(flipped, g, preferred_element_type=F32)
-            return total
-
-        made = lax.fori_loop(0, cols // chunk // group, go, jnp.zeros((tile, width), F32))
+        def make(c):
+            at = pl.ds(c * chunk, chunk)
+            summed = jnp.dot(lead, w_ref[:, at], preferred_element_type=F32)
+            return (e_ref[:, at].astype(F32) * (summed - level)).astype(BF16)
+
+        made = jnp.zeros((tile, width), F32)
+        ahead = make(0)
+        for c in range(cols // chunk):
+            g = ahead
+            if c + 1 < cols // chunk:
+                ahead = make(c + 1)
+            at = pl.ds(c * chunk, chunk)
+            made = made + jnp.dot(g, tgt_ref[at, :], preferred_element_type=F32)
+            total_ref[:, at] += jnp.dot(flipped, g, preferred_element_type=F32)
         gs_ref[...] = made.astype(BF16)
 
         @pl.when(step == tiles - 1)
@@ -454,8 +512,9 @@
     offset = lax.axis_index("row") * vocab_local
     onehot = (tokens[:, None] == offset + jnp.arange(vocab_local, dtype=jnp.int32)[None, :]).astype(BF16)
     looked = jnp.dot(onehot, emission_table, preferred_element_type=F32).astype(BF16)
-    tgt_block, weighted = gather_targets(nrow, looked, backward_rows, tgt_embed)
-    exp_block, reach, peak, sums = first_pass(src_block, tgt_block, weighted)
+    tgt_block, pair_sum = gather_targets(nrow, looked, tgt_embed)
+    exp_block, peak, sums, weighted = exp_pass(nrow, src_block, tgt_block, pair_sum, backward_rows)
+    reach = reach_pass(exp_block, weighted)
     factor = forward_rows.shape[1] * nrow / tokens.shape[0]
     coeffs, share = make_weights(nrow, ncol, factor, peak, sums, reach, forward_all)
     part_src, part_tgt = second_pass(exp_block, coeffs, share, weighted, tgt_block, src_block)

time: 344 us -> 303 us (0.88)
  Pallas kernels: 301 us -> 258 us
  waiting for transfers between devices: 1.39 us -> 5.32 us
    pallas_call x2 -> x3, Pallas kernels: 157 us -> 122 us  [the longest x1 64.2 us: exp_pass(): pl.pallas_call(functools.partial(exp_body, nrow, tiles, chunk), grid=(til...]
    pallas_call x1, Pallas kernels: 75.3 us -> 66.8 us  [second_pass(): pl.pallas_call(body, grid=(tiles,), in_specs=[pl.BlockSpec((tile, cols),...]
    all_gather x1, waiting for transfers between devices: 0.01 us -> 3.94 us  [on_device(): src_block = lax.all_gather(src_embed, 'col', axis=0, tiled=True)]
    unnamed x26 -> x24, local copies, waits for them, and re-layouts: 16.8 us -> 14.7 us
  transfers between devices with their start and end apart: 2 -> 2, of which waited for: 0 -> 1; matrix products, arithmetic and copies ran while one was open for 3% -> 4% of each run, Pallas kernels for 46% -> 40%
where the time goes in v3:
time: 303 us
  Pallas kernels  258 us (85%)
  local copies, waits for them, and re-layouts  14.7 us (5%)
  between operations  14.2 us (5%)
  matrix products  10.7 us (4%)
  waiting for transfers between devices  5.32 us (2%)
    pallas_call x1, Pallas kernels, second_pass(): pl.pallas_call(body, grid=(tiles,), in_specs=[pl.BlockSpec((tile, cols),...  66.8 us
    pallas_call x1, Pallas kernels, exp_pass(): pl.pallas_call(functools.partial(exp_body, nrow, tiles, chunk), grid=(til...  64.2 us
    pallas_call x1, Pallas kernels, scatter_sums(): pl.pallas_call(functools.partial(scatter_body, nrow, ncol), in_specs=[vme...  48.3 us
    pallas_call x1, Pallas kernels, reach_pass(): pl.pallas_call(body, grid=(rows // tile,), in_specs=[pl.BlockSpec((seqs,...  28.9 us
    pallas_call x1, Pallas kernels, gather_targets(): pl.pallas_call(functools.partial(gather_body, nrow), in_specs=[vmem, hbm]...  28.5 us
    pallas_call x1, Pallas kernels, make_weights(): pl.pallas_call(functools.partial(weights_body, nrow, ncol, factor, fit(ro...  20.9 us
    unnamed x24, local copies, waits for them, and re-layouts  14.7 us
    dot_general x1, matrix products, on_device(): jnp.dot(onehot, emission_table, preferred_element_type=F32).astype(BF16)  10.7 us
  transfers between devices with their start and end apart: 2, of which 1 were waited for; matrix products, arithmetic and copies ran while one was open for 4% of the time, Pallas kernels for 40%

profile of v3, /device:TPU:8, one launch (start us, length us, event | category | flops | bytes accessed | tf_op | source)
XLA Modules:
  0.0 302.6 jit_solution(15407382449263484122)
XLA Ops:
  7.2 0.0 all-gather.3.cloned.1.call-start
  7.2 0.7 all-gather.3.cloned.1.call-update
  7.9 0.0 all-gather.5.cloned.1.call-start
  7.9 0.7 all-gather.5.cloned.1.call-update
  8.7 0.0 copy-start.4
  8.7 10.7 %convolution_convert_fusion = bf16[256,8192]{1,0:T(8,128)(2,1)S(1)} fusion(bf16[1024,8192]{1,0:T(8,128)(2,1)} %param.7, s32[1024]{0:T(1024)S(1)} %iota_add_fusion, s32[256]{0:T(256)} %param.6), kind=kOutput, calls=%fused_computation | convolution fusion | flops 4297326592 | bytes 20976640 | tf_op jit(solution)/shard_map/dot_general | solution.py:514
  19.3 0.0 copy-done.4
  19.3 28.5 %gather_targets.1 = (bf16[8,1024,256]{2,1,0:T(8,128)(2,1)S(1)}, bf16[4,32,8192]{2,1,0:T(8,128)(2,1)S(1)}) custom-call(bf16[8,32,8192]{2,1,0:T(8,128)(2,1)S(1)} %bitcast.7, bf16[1024,256]{1,0:T(8,128)(2,1)S(1)} %copy-done.4), custom_call_target="tpu_custom_call" | custom-call | bytes 104857600 | tf_op jit(solution)/shard_map/gather_targets/pallas_call | solution.py:91
  47.8 0.0 copy-start.7
  47.8 2.0 copy-done.7
  49.8 0.0 copy-start.9
  49.8 1.3 copy-done.9
  51.2 3.9 %all-gather.3.cloned.1.call-done.src_ref = bf16[4096,256]{1,0:T(8,128)(2,1)} async-done(((bf16[1024,256]{1,0:T(8,128)(2,1)}), bf16[4096,256]{1,0:T(8,128)(2,1)}) %all-gather.3.cloned.1.call-update) | async-done | bytes 2097168 | tf_op jit(solution)/shard_map/all_gather | solution.py:509
  55.1 64.2 %exp_pass.1 = (bf16[4096,8192]{1,0:T(8,128)(2,1)}, f32[1,4096]{1,0:T(1,128)}, f32[1,4096]{1,0:T(1,128)}, bf16[8,32,8192]{2,1,0:T(8,128)(2,1)}) custom-call(bf16[4096,256]{1,0:T(8,128)(2,1)} %all-gather.3.cloned.1.call-done.src_ref, bf16[8192,256]{1,0:T(8,128)(2,1)} %bitcast.9, bf16[4,32,8192]{2,1,0:T(8,128)(2,1)} %copy-done.9, bf16[32,8192]{1,0:T(8,128)(2,1)} %back.1), custom_call_target="tpu_custom_call" | custom-call | flops 17179869184 | bytes 209715200 | tf_op jit(solution)/shard_map/exp_pass/pallas_call | solution.py:201
  119.3 0.0 copy-start.5
  119.3 0.0 copy-start.6
  119.3 28.9 %reach_pass.1.reach = f32[256,4096]{1,0:T(8,128)} custom-call(bf16[256,8192]{1,0:T(8,128)(2,1)} %bitcast.11, bf16[4096,8192]{1,0:T(8,128)(2,1)} %get-tuple-element.14.e_ref), custom_call_target="tpu_custom_call" | custom-call | flops 17179869184 | bytes 67108864 | tf_op jit(solution)/shard_map/reach_pass/pallas_call | solution.py:256
  148.2 0.0 copy-done.5
  148.2 0.0 copy-done.6
  148.2 0.0 copy-start
  148.2 2.2 copy-done
  150.4 1.6 copy-done.2
  152.0 20.9 %make_weights.1 = (bf16[256,4096]{1,0:T(8,128)(2,1)S(1)}, f32[1,4096]{1,0:T(1,128)S(1)}) custom-call(f32[1,4096]{1,0:T(1,128)S(1)} %copy-done.5, f32[1,4096]{1,0:T(1,128)S(1)} %copy-done.6, f32[256,4096]{1,0:T(8,128)S(1)} %copy-done, bf16[256,4096]{1,0:T(8,128)(2,1)S(1)} %copy-done.2), custom_call_target="tpu_custom_call" | custom-call | bytes 31457280 | tf_op jit(solution)/shard_map/make_weights/pallas_call | solution.py:340
  172.9 0.0 copy-start.8
  172.9 1.3 copy-done.8
  174.2 0.6 copy-done.10
  174.8 66.8 %second_pass.1 = (bf16[4096,256]{1,0:T(8,128)(2,1)}, bf16[8192,256]{1,0:T(8,128)(2,1)}) custom-call(bf16[4096,8192]{1,0:T(8,128)(2,1)} %get-tuple-element.14.e_ref, bf16[256,4096]{1,0:T(8,128)(2,1)} %copy-done.8, f32[1,4096]{1,0:T(1,128)} %copy-done.10, bf16[256,8192]{1,0:T(8,128)(2,1)} %bitcast.12, bf16[8192,256]{1,0:T(8,128)(2,1)} %bitcast.10, ...), custom_call_target="tpu_custom_call" | custom-call | flops 51539607552 | bytes 104857600 | tf_op jit(solution)/shard_map/second_pass/pallas_call | solution.py:412
  241.6 2.2 copy-done.1
  243.8 1.6 copy-done.3
  245.4 48.3 %scatter_sums.1 = (f32[1024,256]{1,0:T(8,128)S(1)}, f32[1024,256]{1,0:T(8,128)S(1)}) custom-call(bf16[4,1024,256]{2,1,0:T(8,128)(2,1)S(1)} %bitcast.8, bf16[8,1024,256]{2,1,0:T(8,128)(2,1)S(1)} %bitcast.6), custom_call_target="tpu_custom_call" | custom-call | bytes 104857600 | tf_op jit(solution)/shard_map/scatter_sums/pallas_call | solution.py:484
  293.8 1.0 copy.10
  294.7 1.0 copy.11
  (6 shorter events, 0.0 us)
Async XLA Ops:
  7.2 47.9 %all-gather.3.cloned.1.call-start = ((), (), s32[]{:S(2)}) async-start(), calls=%async_computation | async-start | bytes 2621440 | tf_op jit(solution)/shard_map/all_gather | solution.py:509
  7.9 140.3 %all-gather.5.cloned.1.call-start = ((), (), s32[]{:S(2)}) async-start(), calls=%async_computation.1 | async-start | bytes 2621440 | tf_op jit(solution)/shard_map/all_gather | solution.py:510
  8.7 10.7 %copy-start.4 = (bf16[1024,256]{1,0:T(8,128)(2,1)S(1)}, bf16[1024,256]{1,0:T(8,128)(2,1)}, u32[]{:S(2)}) copy-start(bf16[1024,256]{1,0:T(8,128)(2,1)} %tgt.1) | copy-start | bytes 1572868
  47.8 2.0 copy-start.7
  49.8 1.3 copy-start.9
  119.3 28.9 %copy-start.5 = (f32[1,4096]{1,0:T(1,128)S(1)}, f32[1,4096]{1,0:T(1,128)}, u32[]{:S(2)}) copy-start(f32[1,4096]{1,0:T(1,128)} %get-tuple-element.15.peak) | copy-start | bytes 49156
  119.3 28.9 %copy-start.6 = (f32[1,4096]{1,0:T(1,128)S(1)}, f32[1,4096]{1,0:T(1,128)}, u32[]{:S(2)}) copy-start(f32[1,4096]{1,0:T(1,128)} %get-tuple-element.16.sums) | copy-start | bytes 49156
  148.2 2.2 copy-start
  150.4 1.6 copy-start.2
  172.9 1.3 copy-start.8
  174.2 0.6 copy-start.10
  241.6 2.2 copy-start.1
  243.8 1.6 copy-start.3
Sparse Core Ops, SparseCore 0:
  9.6 45.4 all-gather.2
  56.7 44.9 all-gather.4

commit v4 on v3

--- a/solution.py
+++ b/solution.py
@@ -162,7 +162,7 @@
             return best, total + jnp.sum(e, axis=1, keepdims=True)
 
         best, total = lax.fori_loop(
-            0, cols // chunk, go, (jnp.full((tile, 1), -jnp.inf, F32), jnp.zeros((tile, 1), F32))
+            0, cols // chunk, go, (jnp.full((tile, 1), -jnp.inf, F32), jnp.zeros((tile, 1), F32)), unroll=2
         )
         new_peak[...] = best
         sum_ref[...] = to_row(total)
@@ -247,11 +247,11 @@
     chunk = fit(cols, 2048)
 
     def body(w_ref, e_ref, reach_ref):
-        total = jnp.zeros(reach_ref.shape, F32)
+        total = jnp.zeros((tile, seqs), F32)
         for c in range(cols // chunk):
             at = pl.ds(c * chunk, chunk)
-            total = total + lax.dot_general(w_ref[:, at], e_ref[:, at], NT, preferred_element_type=F32)
-        reach_ref[...] = total
+            total = total + lax.dot_general(e_ref[:, at], w_ref[:, at], NT, preferred_element_type=F32)
+        reach_ref[...] = total.T
 
     return pl.pallas_call(
         body,

time: 303 us -> 300 us (0.990)
  no operation moved by 1% of the time
where the time goes in v4:
time: 300 us
  Pallas kernels  255 us (85%)
  local copies, waits for them, and re-layouts  14.7 us (5%)
  between operations  14.2 us (5%)
  matrix products  10.7 us (4%)
  waiting for transfers between devices  5.32 us (2%)
    pallas_call x1, Pallas kernels, second_pass(): pl.pallas_call(body, grid=(tiles,), in_specs=[pl.BlockSpec((tile, cols),...  66.8 us
    pallas_call x1, Pallas kernels, exp_pass(): pl.pallas_call(functools.partial(exp_body, nrow, tiles, chunk), grid=(til...  61.2 us
    pallas_call x1, Pallas kernels, scatter_sums(): pl.pallas_call(functools.partial(scatter_body, nrow, ncol), in_specs=[vme...  48.2 us
    pallas_call x1, Pallas kernels, reach_pass(): pl.pallas_call(body, grid=(rows // tile,), in_specs=[pl.BlockSpec((seqs,...  29.2 us
    pallas_call x1, Pallas kernels, gather_targets(): pl.pallas_call(functools.partial(gather_body, nrow), in_specs=[vmem, hbm]...  28.5 us
    pallas_call x1, Pallas kernels, make_weights(): pl.pallas_call(functools.partial(weights_body, nrow, ncol, factor, fit(ro...  21.2 us
    unnamed x24, local copies, waits for them, and re-layouts  14.7 us
    dot_general x1, matrix products, on_device(): jnp.dot(onehot, emission_table, preferred_element_type=F32).astype(BF16)  10.7 us
  transfers between devices with their start and end apart: 2, of which 1 were waited for; matrix products, arithmetic and copies ran while one was open for 4% of the time, Pallas kernels for 40%

profile of v4, /device:TPU:8, one launch (start us, length us, event | category | flops | bytes accessed | tf_op | source)
XLA Modules:
  0.0 300.0 jit_solution(8544227839924086249)
XLA Ops:
  7.2 0.0 all-gather.3.cloned.1.call-start
  7.2 0.7 all-gather.3.cloned.1.call-update
  7.9 0.0 all-gather.5.cloned.1.call-start
  7.9 0.7 all-gather.5.cloned.1.call-update
  8.7 0.0 copy-start.4
  8.7 10.7 %convolution_convert_fusion = bf16[256,8192]{1,0:T(8,128)(2,1)S(1)} fusion(bf16[1024,8192]{1,0:T(8,128)(2,1)} %param.7, s32[1024]{0:T(1024)S(1)} %iota_add_fusion, s32[256]{0:T(256)} %param.6), kind=kOutput, calls=%fused_computation | convolution fusion | flops 4297326592 | bytes 20976640 | tf_op jit(solution)/shard_map/dot_general | solution.py:514
  19.3 0.0 copy-done.4
  19.3 28.5 %gather_targets.1 = (bf16[8,1024,256]{2,1,0:T(8,128)(2,1)S(1)}, bf16[4,32,8192]{2,1,0:T(8,128)(2,1)S(1)}) custom-call(bf16[8,32,8192]{2,1,0:T(8,128)(2,1)S(1)} %bitcast.7, bf16[1024,256]{1,0:T(8,128)(2,1)S(1)} %copy-done.4), custom_call_target="tpu_custom_call" | custom-call | bytes 104857600 | tf_op jit(solution)/shard_map/gather_targets/pallas_call | solution.py:91
  47.8 0.0 copy-start.7
  47.8 2.0 copy-done.7
  49.8 0.0 copy-start.9
  49.8 1.3 copy-done.9
  51.2 3.9 %all-gather.3.cloned.1.call-done.src_ref = bf16[4096,256]{1,0:T(8,128)(2,1)} async-done(((bf16[1024,256]{1,0:T(8,128)(2,1)}), bf16[4096,256]{1,0:T(8,128)(2,1)}) %all-gather.3.cloned.1.call-update) | async-done | bytes 2097168 | tf_op jit(solution)/shard_map/all_gather | solution.py:509
  55.1 61.2 %exp_pass.1 = (bf16[4096,8192]{1,0:T(8,128)(2,1)}, f32[1,4096]{1,0:T(1,128)}, f32[1,4096]{1,0:T(1,128)}, bf16[8,32,8192]{2,1,0:T(8,128)(2,1)}) custom-call(bf16[4096,256]{1,0:T(8,128)(2,1)} %all-gather.3.cloned.1.call-done.src_ref, bf16[8192,256]{1,0:T(8,128)(2,1)} %bitcast.9, bf16[4,32,8192]{2,1,0:T(8,128)(2,1)} %copy-done.9, bf16[32,8192]{1,0:T(8,128)(2,1)} %back.1), custom_call_target="tpu_custom_call" | custom-call | flops 17179869184 | bytes 209715200 | tf_op jit(solution)/shard_map/exp_pass/pallas_call | solution.py:201
  116.3 0.0 copy-start.5
  116.3 0.0 copy-start.6
  116.3 29.2 %reach_pass.1.reach = f32[256,4096]{1,0:T(8,128)} custom-call(bf16[256,8192]{1,0:T(8,128)(2,1)} %bitcast.11, bf16[4096,8192]{1,0:T(8,128)(2,1)} %get-tuple-element.14.e_ref), custom_call_target="tpu_custom_call" | custom-call | flops 17179869184 | bytes 67108864 | tf_op jit(solution)/shard_map/reach_pass/pallas_call | solution.py:256
  145.4 0.0 copy-done.5
  145.4 0.0 copy-done.6
  145.4 0.0 copy-start
  145.5 2.2 copy-done
  147.6 1.6 copy-done.2
  149.2 21.2 %make_weights.1 = (bf16[256,4096]{1,0:T(8,128)(2,1)S(1)}, f32[1,4096]{1,0:T(1,128)S(1)}) custom-call(f32[1,4096]{1,0:T(1,128)S(1)} %copy-done.5, f32[1,4096]{1,0:T(1,128)S(1)} %copy-done.6, f32[256,4096]{1,0:T(8,128)S(1)} %copy-done, bf16[256,4096]{1,0:T(8,128)(2,1)S(1)} %copy-done.2), custom_call_target="tpu_custom_call" | custom-call | bytes 31457280 | tf_op jit(solution)/shard_map/make_weights/pallas_call | solution.py:340
  170.5 0.0 copy-start.8
  170.5 1.3 copy-done.8
  171.8 0.6 copy-done.10
  172.4 66.8 %second_pass.1 = (bf16[4096,256]{1,0:T(8,128)(2,1)}, bf16[8192,256]{1,0:T(8,128)(2,1)}) custom-call(bf16[4096,8192]{1,0:T(8,128)(2,1)} %get-tuple-element.14.e_ref, bf16[256,4096]{1,0:T(8,128)(2,1)} %copy-done.8, f32[1,4096]{1,0:T(1,128)} %copy-done.10, bf16[256,8192]{1,0:T(8,128)(2,1)} %bitcast.12, bf16[8192,256]{1,0:T(8,128)(2,1)} %bitcast.10, ...), custom_call_target="tpu_custom_call" | custom-call | flops 51539607552 | bytes 104857600 | tf_op jit(solution)/shard_map/second_pass/pallas_call | solution.py:412
  239.2 2.2 copy-done.1
  241.4 1.6 copy-done.3
  243.0 48.2 %scatter_sums.1 = (f32[1024,256]{1,0:T(8,128)S(1)}, f32[1024,256]{1,0:T(8,128)S(1)}) custom-call(bf16[4,1024,256]{2,1,0:T(8,128)(2,1)S(1)} %bitcast.8, bf16[8,1024,256]{2,1,0:T(8,128)(2,1)S(1)} %bitcast.6), custom_call_target="tpu_custom_call" | custom-call | bytes 104857600 | tf_op jit(solution)/shard_map/scatter_sums/pallas_call | solution.py:484
  291.2 1.0 copy.10
  292.2 1.0 copy.11
  (6 shorter events, 0.0 us)
Async XLA Ops:
  7.2 47.9 %all-gather.3.cloned.1.call-start = ((), (), s32[]{:S(2)}) async-start(), calls=%async_computation | async-start | bytes 2621440 | tf_op jit(solution)/shard_map/all_gather | solution.py:509
  7.9 137.5 %all-gather.5.cloned.1.call-start = ((), (), s32[]{:S(2)}) async-start(), calls=%async_computation.1 | async-start | bytes 2621440 | tf_op jit(solution)/shard_map/all_gather | solution.py:510
  8.7 10.7 %copy-start.4 = (bf16[1024,256]{1,0:T(8,128)(2,1)S(1)}, bf16[1024,256]{1,0:T(8,128)(2,1)}, u32[]{:S(2)}) copy-start(bf16[1024,256]{1,0:T(8,128)(2,1)} %tgt.1) | copy-start | bytes 1572868
  47.8 2.0 copy-start.7
  49.8 1.3 copy-start.9
  116.3 29.2 %copy-start.5 = (f32[1,4096]{1,0:T(1,128)S(1)}, f32[1,4096]{1,0:T(1,128)}, u32[]{:S(2)}) copy-start(f32[1,4096]{1,0:T(1,128)} %get-tuple-element.15.peak) | copy-start | bytes 49156
  116.3 29.2 %copy-start.6 = (f32[1,4096]{1,0:T(1,128)S(1)}, f32[1,4096]{1,0:T(1,128)}, u32[]{:S(2)}) copy-start(f32[1,4096]{1,0:T(1,128)} %get-tuple-element.16.sums) | copy-start | bytes 49156
  145.4 2.2 copy-start
  147.6 1.6 copy-start.2
  170.5 1.3 copy-start.8
  171.8 0.6 copy-start.10
  239.2 2.2 copy-start.1
  241.4 1.6 copy-start.3
Sparse Core Ops, SparseCore 0:
  9.6 45.4 all-gather.2
  56.7 44.8 all-gather.4
